TPU v7x, 256 devices: a whole 4x4x8 slice. The times are simulated.
256 devices in a mesh: pool: 8 (over z), ctx: 4 (over x), head: 8 (over y, core).
Axes of the slice: x: 4, y: 4, z: 8, core: 2. Of those that a mesh axis runs over, the one named last changes fastest.
Arguments:
- query_nope: bfloat16 [5120, 4096], P(('pool', 'ctx'), 'head'), may hold values from -6 to 6
- query_rope: bfloat16 [5120, 2048], P(('pool', 'ctx'), 'head'), may hold values from -100 to 100
- new_latent: bfloat16 [2560, 1152], P(('pool', 'ctx')), may hold values from -6 to 6
- cache_pool: bfloat16 [512, 73728], P(('pool', 'ctx')), may hold values from -6 to 6
- hit_holder: int32 [8, 64], replicated, may hold values from 0 to 31, as said below
- hit_block: int32 [8, 64], replicated, may hold values from 0 to 15
- prior_blocks: int32 [8, 2], replicated, may hold values from 1 to 63, as said below
- new_counts: int32 [8, 2], replicated, may hold values from 1 to 480, 640 in all within a row
- key_absorb: bfloat16 [32, 128, 512], P('head'), may hold values from -0.5 to 0.5
- value_absorb: bfloat16 [32, 512, 128], P('head'), may hold values from -1 to 1
- out_weight: bfloat16 [4096, 7168], P('head'), may hold values from -0.375 to 0.375
Outputs:
- layer_output: bfloat16 [5120, 7168], P(('pool', 'ctx'), 'head')
Inputs may be any that keep to these rules, and one draw needn't show every extreme that they name: `hit_holder`: row g lists group g's cached blocks, request 0's first; among the listed blocks of a group each holder appears at most 2 times, and in some group every holder appears exactly 2 times; entries past a group's blocks are ignored. `prior_blocks`: A group's blocks, the sum of its row, number at most 64, and exactly that in some group.
All inputs are finite; a program needn't handle non-finite values.
Results may differ from a plain program's by a relative error of at most 0.0086.
Values may be sent and summed in bfloat16 or wider, within the bound.
No kernel may reach another device: no remote copies, remote signals or barrier semaphores. Data moves between devices by JAX's collectives and lax.ppermute only.
A program may use at most 128 MiB of HBM per device.

v0:
```python
from functools import partial

import jax
import jax.numpy as jnp
from jax import lax
from jax.experimental import pallas as pl
from jax.experimental.pallas import tpu as pltpu
from jax.sharding import PartitionSpec as P

KV_RANK = 512
ROPE = 64
QK_NOPE = 128
VD = 128
BLK = 128
PAIRS = BLK // 2
WIDE2 = 2 * (KV_RANK + ROPE)
HEADS = 4
TOK = 160
SLOTS = 16
KEYS = SLOTS * BLK
CUT = 96
KW = 768
BIG = 2.0**100
SCALE = (QK_NOPE + ROPE) ** (-0.5)
LOG2E = 1.4426950408889634
BF = jnp.bfloat16
F32 = jnp.float32
STAT = 16
ORDER = (0, 3, 1, 2)


def iota(shape, dim):
    return lax.broadcasted_iota(jnp.int32, shape, dim)


def pick_kernel(
    ids, prior, cache_ref, holder_ref, block_ref, nope_ref, rope_ref, out_ref, query_ref
):
    query_ref[:, 0:512] = nope_ref[...]
    query_ref[:, 512:768] = rope_ref[...]
    me = ids[0] * 4 + ids[1]
    core = ids[2] & 1
    lane = iota((8, 64), 1)
    group = iota((8, 64), 0)
    count = jnp.zeros((8, 64), jnp.int32)
    for g in range(8):
        count = jnp.where(group == g, prior[0, g] + prior[1, g], count)
    match = (holder_ref[...] == me) & (lane < count)
    first = jnp.min(jnp.where(match, lane, 1000), axis=1, keepdims=True)
    last = jnp.max(jnp.where(match, lane, -1), axis=1, keepdims=True)
    wanted = jnp.where(core == 0, first, jnp.where(last > first, last, -2))
    chosen = match & (lane == wanted)
    index = jnp.sum(jnp.where(chosen, block_ref[...] + 1, 0), axis=1, keepdims=True) - 1
    spread = (iota((128, 8), 0) // 16 == iota((128, 8), 1)).astype(BF)
    rows_index = jnp.dot(
        spread,
        jnp.broadcast_to(index.astype(F32), (8, 256)).astype(BF),
        preferred_element_type=F32,
    )
    row = iota((128, 256), 0)
    col = iota((128, 256), 1)
    onehot = ((col // 16 == row % 16) & ((col % 16).astype(F32) == rows_index)).astype(BF)
    for part in range(2):
        stacked = jnp.concatenate(
            [
                cache_ref[:, p * WIDE2 : (p + 1) * WIDE2]
                for p in range(part * 16, part * 16 + 16)
            ],
            axis=0,
        )
        out = jnp.dot(onehot, stacked, preferred_element_type=F32).astype(BF)
        even, odd, rope = align(out)
        to = slice(part * 16, part * 16 + 16)
        for g in range(8):
            at = slice(g * 16, (g + 1) * 16)
            for j in range(4):
                out_ref[g, to, j * 128 : (j + 1) * 128] = even[j][at]
                out_ref[g, to, 512 + j * 128 : 640 + j * 128] = odd[j][at]
            out_ref[g, to, 1024:1152] = rope[at]


def align(rows):
    low = iota((rows.shape[0], 128), 1) < 64
    tile = [rows[:, j * 128 : (j + 1) * 128] for j in range(9)]
    flip = {j: pltpu.roll(tile[j].astype(F32), 64, 1).astype(BF) for j in range(5, 9)}
    flip[4] = pltpu.roll(tile[4].astype(F32), 64, 1).astype(BF)
    odd = [jnp.where(low, flip[4 + j], flip[5 + j]) for j in range(4)]
    return tile[:4], odd, jnp.where(low, tile[4], tile[8])


def both_ropes(tile):
    low = iota(tile.shape, 1) < 64
    flip = pltpu.roll(tile.astype(F32), 64, 1).astype(BF)
    return jnp.where(low, tile, flip), jnp.where(low, flip, tile)


def wide(value, n):
    return jnp.concatenate([value] * (n // 128), axis=1)


def turn_of(step):
    return jnp.where(step == 0, 0, jnp.where(step == 1, 3, jnp.where(step == 2, 1, 2)))


def product(queries, keys):
    return lax.dot_general(
        queries, keys, (((1,), (1,)), ((), ())), preferred_element_type=F32
    )


def ready_kernel(
    ids, holder, prior, counts,
    q0, qm, qp, qx, qy, ka_ref, nl_ref,
    q_out, acc_out, mx_out, sm_out, mark_out, table,
    part, kn, seen,
):
    step = pl.program_id(0)
    group = ids[0]
    ctx = ids[1]
    n0 = counts[0, group]

    def mark(n, base, keys0, keys1):
        row = iota((n, 128), 0) + base
        lane = iota((n, 128), 1)
        miss0 = (lane == 0) & jnp.logical_not(keys0(row))
        miss1 = (lane == 1) & jnp.logical_not(keys1(row))
        return jnp.where(miss0 | miss1, -BIG, 0.0).astype(BF)

    @pl.when(step == 0)
    def _():
        for i in range(SLOTS):
            table[i] = -1
        for i in range(8):
            seen[i] = 0
        own = prior[0, group]
        total = own + prior[1, group]

        def entry(e, carry):
            filled, mine = carry
            where = holder[group, e]
            hit = (where & 3) == ctx
            p = where >> 2

            @pl.when(hit)
            def _():
                s = seen[p]
                seen[p] = s + 1
                table[p * 2 + s] = filled

            add = hit.astype(jnp.int32)
            return filled + add, mine + jnp.where(e < own, add, 0)

        filled, mine = lax.fori_loop(0, total, entry, (jnp.int32(0), jnp.int32(0)))
        end0 = mine * BLK
        end1 = filled * BLK
        table[SLOTS] = end0
        table[SLOTS + 1] = end1
        table[SLOTS + 2] = n0
        for i in range(SLOTS + 3, 32):
            table[i] = 0
        for i in range(SLOTS):
            dead = table[i] < 0

            @pl.when(dead)
            def _():
                table[i] = filled

            filled = filled + dead.astype(jnp.int32)

        def marks(i, _):
            at = pl.multiple_of(i * BLK, BLK)
            mark_out[pl.ds(at, BLK), :] = mark(
                BLK, at, lambda r: r < end0, lambda r: (r >= end0) & (r < end1)
            )
            return 0

        lax.fori_loop(0, SLOTS, marks, 0)

        even, odd, rope = align(nl_ref[...])
        rope = both_ropes(rope)
        kn[...] = jnp.zeros(kn.shape, BF)
        for parity, latent in enumerate((even, odd)):
            at = slice(parity * 128, parity * 128 + 80)
            for j in range(4):
                kn[at, j * 128 : (j + 1) * 128] = latent[j]
            kn[at, 512:640] = rope[parity]

        def new_position(row):
            return ctx * TOK + 2 * (row & 127) + (row >> 7)

        kn[:, 640:768] = mark(
            256, 0, lambda r: new_position(r) < n0, lambda r: new_position(r) >= n0
        )
        part[...] = q0[...]

    @pl.when(step == 1)
    def _():
        part[...] = qm[...]

    @pl.when(step == 2)
    def _():
        part[...] = qp[...]

    @pl.when(step == 3)
    def _():
        part[0:80] = qx[...]
        part[80:160] = qy[...]

    rows = HEADS * TOK
    t0 = ((ctx + turn_of(step)) & 3) * TOK
    lane = iota((TOK, 128), 1)
    token = iota((TOK, 128), 0) + t0
    flags = jnp.where(
        ((lane == 0) & (token < n0)) | ((lane == 1) & (token >= n0)), 1.0, 0.0
    ).astype(BF)
    for j in range(HEADS):
        at = slice(j * TOK, (j + 1) * TOK)
        q_out[0, at, 0:512] = jnp.dot(
            part[:, j * 128 : (j + 1) * 128], ka_ref[j], preferred_element_type=F32
        ).astype(BF)
        rope = part[:, 512 + (j // 2) * 128 : 640 + (j // 2) * 128]
        keep = lane < 64 if j % 2 == 0 else lane >= 64
        q_out[0, at, 512:640] = jnp.where(keep, rope, jnp.zeros_like(rope))
        q_out[0, at, 640:768] = flags

    visible = t0 + TOK > ctx * TOK

    @pl.when(visible)
    def _():
        key = iota((rows, 256), 1)
        position = ctx * TOK + 2 * (key & 127) + (key >> 7)
        here = jnp.concatenate([iota((TOK, 256), 0)] * HEADS, axis=0) + t0
        seen_keys = (position <= here) & ((key & 127) < 80)
        scores = jnp.where(seen_keys, product(q_out[0], kn[...]), -BIG)
        top = jnp.maximum(
            jnp.full((rows, 128), -BIG, F32), jnp.max(scores, axis=1, keepdims=True)
        )
        weight = jnp.exp2((scores - wide(top, 256)) * (SCALE * LOG2E))
        mx_out[0] = top
        sm_out[0] = jnp.zeros((rows, 128), F32) + jnp.sum(weight, axis=1, keepdims=True)
        acc_out[0] = jnp.dot(weight.astype(BF), kn[:, 0:512], preferred_element_type=F32)

    @pl.when(jnp.logical_not(visible))
    def _():
        mx_out[0] = jnp.full((rows, 128), -BIG, F32)
        sm_out[0] = jnp.zeros((rows, 128), F32)
        acc_out[0] = jnp.zeros((rows, 512), F32)


def attend_kernel(
    ids, table,
    q_ref, acc0, mx0, sm0, va_ref, mark_ref, a0, am, ap, b0, bm, bp,
    far_a, far_b, low_ref, high_ref, kept_ref,
    kc, kb, acc, mx, sm, sem,
):
    step = pl.program_id(0)
    core = ids[2] & 1
    end0 = table[SLOTS]
    end1 = table[SLOTS + 1]
    n0 = table[SLOTS + 2]

    @pl.when(step == 0)
    def _():
        marks = pltpu.make_async_copy(mark_ref, kb.at[:, pl.ds(640, 128)], sem.at[2])
        marks.start()
        for w, (own, first, second) in enumerate(((a0, am, ap), (b0, bm, bp))):
            pltpu.make_async_copy(own, kc.at[w, 0], sem.at[w]).start()
            pltpu.make_async_copy(first, kc.at[w, 1, pl.ds(0, 4)], sem.at[w]).start()
            pltpu.make_async_copy(second, kc.at[w, 1, pl.ds(4, 4)], sem.at[w]).start()
        for w in range(2):
            pltpu.make_async_copy(kc.at[w], kc.at[w], sem.at[w]).wait()
            slot = core if w == 0 else 1 - core

            def shape_up(p, _):
                at = table[p * 2 + slot] * BLK
                for half in range(2):
                    block = kc[w, half, p]
                    ropes = both_ropes(block[:, 1024:1152])
                    for parity in range(2):
                        to = pl.ds(pl.multiple_of(at + half * 64 + parity * 32, 32), 32)
                        kb[to, 0:512] = block[:, parity * 512 : parity * 512 + 512]
                        kb[to, 512:640] = ropes[parity]
                return 0

            lax.fori_loop(0, 8, shape_up, 0)
        marks.wait()

    t0 = ((ids[1] + turn_of(step)) & 3) * TOK
    low = jnp.where(t0 < n0, 0, end0)
    high = jnp.where(t0 + TOK > n0, end1, end0)
    extent = high - low

    def chunk(size):
        at = pl.ds(pl.multiple_of(jnp.minimum(low, KEYS - size), BLK), size)
        scores = product(q_ref[0], kb[at, :])
        before = mx0[0]
        top = jnp.maximum(before, jnp.max(scores, axis=1, keepdims=True))
        keep = jnp.exp2((before - top) * (SCALE * LOG2E))
        weight = jnp.exp2((scores - wide(top, size)) * (SCALE * LOG2E))
        mx[...] = top
        sm[...] = sm0[0] * keep + jnp.sum(weight, axis=1, keepdims=True)
        acc[...] = acc0[0] * wide(keep, 512) + jnp.dot(
            weight.astype(BF), kb[at, 0:512], preferred_element_type=F32
        )

    sizes = (0, 128, 512, 1024, 1536, 2048)
    for small, size in zip(sizes, sizes[1:]):

        @pl.when((extent > small) & (extent <= size))
        def _():
            chunk(size)

    @pl.when(extent <= 0)
    def _():
        acc[...], mx[...], sm[...] = acc0[0], mx0[0], sm0[0]

    lane16 = iota((16, 128), 1)
    stats = jnp.zeros((16, 128), F32)
    heads = []
    for j in range(HEADS):
        at = slice(j * TOK, (j + 1) * TOK)
        mass = sm[at, :]
        none = mass == 0.0
        safe = jnp.where(none, 1.0, mass)
        lse = jnp.where(none, -BIG, mx[at, :] * SCALE + jnp.log(safe))
        latent = (acc[at, :] * wide(1.0 / safe, 512)).astype(BF)
        heads.append(jnp.dot(latent, va_ref[j], preferred_element_type=F32).astype(BF))
        one = lse.astype(BF).astype(F32)
        two = (lse - one).astype(BF).astype(F32)
        three = lse - one - two
        for k in range(TOK // 16):
            base = 12 * k + 3 * j
            cut = slice(k * 16, (k + 1) * 16)
            for i, value in enumerate((one, two, three)):
                stats = jnp.where(lane16 == base + i, value[cut], stats)

    def emit(out_ref, first, count):
        for j in range(HEADS):
            out_ref[0:count, j * 128 : (j + 1) * 128] = heads[j][first : first + count]
        if first + count == TOK:
            out_ref[count : count + STAT, 0:128] = stats.astype(BF)
            out_ref[count : count + STAT, 128:512] = jnp.zeros((STAT, 384), BF)

    for turn, parts in (
        (0, ((kept_ref, 0, TOK),)),
        (1, ((high_ref, 0, TOK),)),
        (2, ((far_a, 0, CUT), (far_b, CUT, TOK - CUT))),
        (3, ((low_ref, 0, TOK),)),
    ):

        @pl.when(step == ORDER.index(turn))
        def _():
            for part in parts:
                emit(*part)


def merge(kept, low, high, far_a, far_b):
    lane_in = iota((128, 512), 0)
    lane_head = iota((128, 512), 1) // 128
    outs = []
    tails = [ref[TOK : TOK + STAT, 0:128] for ref in (kept, low, high)]
    stats = jnp.concatenate([*tails, far_b[TOK - CUT : TOK - CUT + STAT, 0:128]], axis=0)
    for k in range(TOK // 16):
        pickup = ((lane_in >= 12 * k + 3 * lane_head) & (lane_in < 12 * k + 3 * lane_head + 3))
        lse = jnp.dot(stats, pickup.astype(BF), preferred_element_type=F32)
        lse = [lse[c * 16 : (c + 1) * 16] for c in range(4)]
        top = jnp.maximum(jnp.maximum(lse[0], lse[1]), jnp.maximum(lse[2], lse[3]))
        weight = [jnp.exp(v - top) for v in lse]
        total = weight[0] + weight[1] + weight[2] + weight[3]
        at = slice(k * 16, (k + 1) * 16)
        far = far_a[at, :] if k * 16 < CUT else far_b[k * 16 - CUT : k * 16 - CUT + 16, :]
        values = (kept[at, :], low[at, :], high[at, :], far)
        mixed = sum(w * v.astype(F32) for w, v in zip(weight, values))
        outs.append((mixed / total).astype(BF))
    return outs


def fetch(ids, w_ref, held, sem, picks):
    copies = []
    for i, (turn, other) in enumerate(picks):
        y = ((ids[2] >> 1) + turn) & 3
        column = (y * 2 + ((ids[2] & 1) ^ other)) * 896
        copies.append(
            pltpu.make_async_copy(
                w_ref.at[:, pl.ds(pl.multiple_of(column, 128), 896)], held.at[i], sem.at[i]
            )
        )
        copies[-1].start()
    return copies


def first_kernel(ids, g0, g1, g2, g3, g4, w_ref, head_ref, away_ref, home_ref, held, sem):
    copies = fetch(ids, w_ref, held, sem, ((2, 1), (2, 0)))
    for k, value in enumerate(merge(g0, g1, g2, g3, g4)):
        head_ref[k * 16 : (k + 1) * 16, :] = value
    for i, out in enumerate((away_ref, home_ref)):
        copies[i].wait()
        out[...] = jnp.dot(head_ref[...], held[i], preferred_element_type=F32).astype(BF)


def rest_kernel(other, ids, head_ref, w_ref, out_ref, held, sem):
    copies = fetch(ids, w_ref, held, sem, ((1, other), (3, other), (0, other)))
    for i in range(3):
        copies[i].wait()
        out_ref[i] = jnp.dot(head_ref[...], held[i], preferred_element_type=F32).astype(BF)


def shift(value, axis, by, size):
    return lax.ppermute(value, axis, [(i, (i + by) % size) for i in range(size)])


def swap_core(value):
    return lax.ppermute(value, "head", [(i, i ^ 1) for i in range(8)])


def whole(*shape):
    return pl.BlockSpec(shape, lambda i, *_: (0,) * len(shape))


def prepare(ids, hit_holder, prior_blocks, new_counts, queries, key_absorb, new_latent):
    rows = HEADS * TOK
    tile = lambda n: pl.BlockSpec((1, rows, n), lambda i, *_: (i, 0, 0))
    return pl.pallas_call(
        ready_kernel,
        grid_spec=pltpu.PrefetchScalarGridSpec(
            num_scalar_prefetch=4,
            grid=(4,),
            in_specs=[
                whole(TOK, 768), whole(TOK, 768), whole(TOK, 768), whole(80, 768), whole(80, 768),
                whole(HEADS, 128, 512),
                whole(80, WIDE2),
            ],
            out_specs=[
                tile(KW), tile(512), tile(128), tile(128),
                whole(KEYS, 128),
                pl.BlockSpec(memory_space=pltpu.SMEM),
            ],
            scratch_shapes=[
                pltpu.VMEM((TOK, 768), BF),
                pltpu.VMEM((256, KW), BF),
                pltpu.SMEM((8,), jnp.int32),
            ],
        ),
        out_shape=[
            pltpu.HBM((4, rows, KW), BF),
            pltpu.HBM((4, rows, 512), F32),
            pltpu.HBM((4, rows, 128), F32),
            pltpu.HBM((4, rows, 128), F32),
            pltpu.HBM((KEYS, 128), BF),
            jax.ShapeDtypeStruct((32,), jnp.int32),
        ],
        compiler_params=pltpu.CompilerParams(vmem_limit_bytes=28 * 2**20),
        cost_estimate=pl.CostEstimate(
            flops=3 * 10**9, bytes_accessed=14 * 10**6, transcendentals=10**6
        ),
        name="prepare",
    )(ids, hit_holder, prior_blocks, new_counts, *queries, key_absorb, new_latent)


def attend(ids, ready, pieces, value_absorb):
    q_all, acc0, mx0, sm0, marks = [
        pltpu.with_memory_space_constraint(value, pltpu.HBM) for value in ready[:5]
    ]
    rows = HEADS * TOK
    tile = lambda n: pl.BlockSpec((1, rows, n), lambda i, *_: (i, 0, 0))
    out_rows = (CUT, TOK - CUT + STAT, TOK + STAT, TOK + STAT, TOK + STAT)
    return pl.pallas_call(
        attend_kernel,
        grid_spec=pltpu.PrefetchScalarGridSpec(
            num_scalar_prefetch=2,
            grid=(4,),
            in_specs=[tile(KW), tile(512), tile(128), tile(128), whole(HEADS, 512, 128)]
            + [pl.BlockSpec(memory_space=pl.ANY)] * 7,
            out_specs=[whole(n, 512) for n in out_rows],
            scratch_shapes=[
                pltpu.VMEM((2, 2, 8, 32, WIDE2), BF),
                pltpu.VMEM((KEYS, KW), BF),
                pltpu.VMEM((rows, 512), F32),
                pltpu.VMEM((rows, 128), F32),
                pltpu.VMEM((rows, 128), F32),
                pltpu.SemaphoreType.DMA((3,)),
            ],
        ),
        out_shape=[jax.ShapeDtypeStruct((n, 512), BF) for n in out_rows],
        compiler_params=pltpu.CompilerParams(vmem_limit_bytes=40 * 2**20),
        cost_estimate=pl.CostEstimate(
            flops=12 * 10**9, bytes_accessed=15 * 10**6, transcendentals=5 * 10**6
        ),
        name="attend",
    )(ids, ready[5], q_all, acc0, mx0, sm0, value_absorb, marks, *pieces)


def rest(other, ids, heads, out_weight):
    return pl.pallas_call(
        partial(rest_kernel, other),
        grid_spec=pltpu.PrefetchScalarGridSpec(
            num_scalar_prefetch=1,
            grid=(1,),
            in_specs=[whole(TOK, 512), pl.BlockSpec(memory_space=pl.ANY)],
            out_specs=whole(3, TOK, 896),
            scratch_shapes=[pltpu.VMEM((3, 512, 896), BF), pltpu.SemaphoreType.DMA((3,))],
        ),
        out_shape=jax.ShapeDtypeStruct((3, TOK, 896), BF),
        compiler_params=pltpu.CompilerParams(vmem_limit_bytes=12 * 2**20),
        cost_estimate=pl.CostEstimate(
            flops=1 * 10**9, bytes_accessed=4 * 10**6, transcendentals=0
        ),
        name="project_home" if other == 0 else "project_away",
    )(ids, heads, out_weight)


def local(
    query_nope, query_rope, new_latent, cache_pool, hit_holder, hit_block,
    prior_blocks, new_counts, key_absorb, value_absorb, out_weight,
):
    ids = jnp.stack(
        [lax.axis_index("pool"), lax.axis_index("ctx"), lax.axis_index("head")]
    ).astype(jnp.int32)

    half = 32 * WIDE2
    prior = prior_blocks.T
    counts = new_counts.T
    picked, queries = pl.pallas_call(
        pick_kernel,
        grid_spec=pltpu.PrefetchScalarGridSpec(
            num_scalar_prefetch=2,
            grid=(1,),
            in_specs=[
                pl.BlockSpec((16, half), lambda i, ids, _: (0, (ids[2] >> 1) & 1)),
                whole(8, 64),
                whole(8, 64),
                whole(TOK, 512),
                whole(TOK, 256),
            ],
            out_specs=[whole(8, 32, WIDE2), whole(TOK, 768)],
        ),
        out_shape=[
            jax.ShapeDtypeStruct((8, 32, WIDE2), BF),
            jax.ShapeDtypeStruct((TOK, 768), BF),
        ],
        name="pick_blocks",
    )(ids, prior, cache_pool, hit_holder, hit_block, query_nope, query_rope)

    qm = shift(queries, "ctx", 1, 4)
    qp = shift(queries, "ctx", -1, 4)
    qx = shift(qm[:80], "ctx", 1, 4)
    qy = shift(qp[80:], "ctx", -1, 4)

    a0 = lax.all_to_all(picked, "pool", split_axis=0, concat_axis=0, tiled=True)

    a0, qx, qy = lax.optimization_barrier((a0, qx, qy))
    am = shift(a0[:4], "head", 2, 8)
    ap = shift(a0[4:], "head", -2, 8)
    b0 = swap_core(a0)
    ready = prepare(
        ids, hit_holder, prior, counts, (queries, qm, qp, qx, qy), key_absorb, new_latent
    )
    table, am, ap, b0 = lax.optimization_barrier((ready[5], am, ap, b0))
    bm = swap_core(am)
    bp = swap_core(ap)
    far_a, far_b, to_low, to_high, kept = attend(
        ids, (*ready[:5], table), (a0, am, ap, b0, bm, bp), value_absorb
    )
    far_b = shift(far_b, "ctx", -1, 4)
    far_a = shift(far_a, "ctx", 2, 4)
    from_low = shift(to_high, "ctx", 1, 4)
    from_high = shift(to_low, "ctx", -1, 4)
    far_b = shift(far_b, "ctx", -1, 4)

    heads, away2, home2 = pl.pallas_call(
        first_kernel,
        grid_spec=pltpu.PrefetchScalarGridSpec(
            num_scalar_prefetch=1,
            grid=(1,),
            in_specs=[whole(TOK + STAT, 512)] * 3
            + [whole(CUT, 512), whole(TOK - CUT + STAT, 512)]
            + [pl.BlockSpec(memory_space=pl.ANY)],
            out_specs=[whole(TOK, 512), whole(TOK, 896), whole(TOK, 896)],
            scratch_shapes=[pltpu.VMEM((2, 512, 896), BF), pltpu.SemaphoreType.DMA((2,))],
        ),
        out_shape=[
            jax.ShapeDtypeStruct((TOK, 512), BF),
            jax.ShapeDtypeStruct((TOK, 896), BF),
            jax.ShapeDtypeStruct((TOK, 896), BF),
        ],
        compiler_params=pltpu.CompilerParams(vmem_limit_bytes=12 * 2**20),
        name="merge_project",
    )(ids, kept, from_low, from_high, far_a, far_b, out_weight)
    across = swap_core(away2)
    opposite = home2.astype(F32) + across.astype(F32)
    part_a = opposite[:80].astype(BF)
    part_b = opposite[80:].astype(BF)
    heads, part_a, part_b = lax.optimization_barrier((heads, part_a, part_b))
    part_a = shift(part_a, "head", 2, 8)
    part_b = shift(part_b, "head", -2, 8)
    away = rest(1, ids, heads, out_weight)
    arrived = swap_core(away)
    home = rest(0, ids, heads, out_weight)
    both = home.astype(F32) + arrived.astype(F32)
    up = jnp.concatenate([both[0, :80] + part_a.astype(F32), both[0, 80:]], axis=0).astype(BF)
    down = jnp.concatenate([both[1, :80], both[1, 80:] + part_b.astype(F32)], axis=0).astype(BF)
    got_up = shift(up, "head", 2, 8)
    got_down = shift(down, "head", -2, 8)
    return (both[2] + got_up.astype(F32) + got_down.astype(F32)).astype(BF)


def solution(mesh):
    return jax.shard_map(
        local,
        mesh=mesh,
        in_specs=(
            P(("pool", "ctx"), "head"),
            P(("pool", "ctx"), "head"),
            P(("pool", "ctx"), None),
            P(("pool", "ctx"), None),
            P(),
            P(),
            P(),
            P(),
            P("head", None, None),
            P("head", None, None),
            P("head", None),
        ),
        out_specs=P(("pool", "ctx"), "head"),
        check_vma=False,
    )
```

profile of v0, /device:TPU:32, one launch (start us, length us, event | category | flops | bytes accessed | tf_op | source)
XLA Modules:
  0.0 107.2 jit_solution(7641586887278505626)
XLA Ops:
  0.7 3.7 %pick_blocks.1 = (bf16[8,32,1152]{2,1,0:T(8,128)(2,1)}, bf16[160,768]{1,0:T(8,128)(2,1)}) custom-call(s32[3]{0:T(128)} %pad_add_fusion.ids, s32[2,8]{1,0:T(2,128)} %bitcast.31, bf16[16,73728]{1,0:T(8,128)(2,1)} %cache_ref.1, s32[8,64]{1,0:T(8,128)} %holder.1, s32[8,64]{1,0:T(8,128)} %block_ref.1, bf16[160,512]{1,0:T(8,128)(2,1)} %nope_ref.1, ...), custom_call_target="tpu_custom_call" | custom-call | tf_op jit(solution)/shard_map/pick_blocks/pallas_call | solution.py:523
  4.5 8.7 %all-to-all-start = ((bf16[8,32,1152]{2,1,0:T(8,128)(2,1)}), bf16[8,32,1152]{2,1,0:T(8,128)(2,1)S(1)}, u32[]{:S(2)}, u32[]{:S(2)}) async-start(bf16[8,32,1152]{2,1,0:T(8,128)(2,1)} %get-tuple-element.32), calls=%async_computation | async-start | bytes 1179648 | tf_op jit(solution)/shard_map/all_to_all | solution.py:549
  13.2 2.8 %collective-permute-start.1 = (bf16[160,768]{1,0:T(8,128)(2,1)}, bf16[160,768]{1,0:T(8,128)(2,1)S(1)}, u32[]{:S(2)}, u32[]{:S(2)}) collective-permute-start(bf16[160,768]{1,0:T(8,128)(2,1)} %get-tuple-element.31.q0), channel_id=1, source_target_pairs={{0,24},{8,0},{16,8},{24,16},{1,25},{9,1},{17,9},{25,17},{2,26},{10... | collective-permute-start | bytes 737288 | tf_op jit(solution)/shard_map/ppermute | solution.py:409
  16.0 5.0 %collective-permute-done.1.qp = bf16[160,768]{1,0:T(8,128)(2,1)S(1)} collective-permute-done((bf16[160,768]{1,0:T(8,128)(2,1)}, bf16[160,768]{1,0:T(8,128)(2,1)S(1)}, u32[]{:S(2)}, u32[]{:S(2)}) %collective-permute-start.1) | collective-permute-done | bytes 245792 | tf_op jit(solution)/shard_map/ppermute | solution.py:409
  20.9 3.7 %collective-permute-start.3 = (bf16[80,768]{1,0:T(8,128)(2,1)S(1)}, bf16[80,768]{1,0:T(8,128)(2,1)S(1)}, u32[]{:S(2)}, u32[]{:S(2)}) collective-permute-start(bf16[80,768]{1,0:T(8,128)(2,1)S(1)} %slice.49), channel_id=1, source_target_pairs={{0,24},{8,0},{16,8},{24,16},{1,25},{9,1},{17,9},{25,17},{2,26},{10... | collective-permute-start | bytes 368648 | tf_op jit(solution)/shard_map/ppermute | solution.py:409
  24.7 2.3 %collective-permute-done.3.qy = bf16[80,768]{1,0:T(8,128)(2,1)S(1)} collective-permute-done((bf16[80,768]{1,0:T(8,128)(2,1)S(1)}, bf16[80,768]{1,0:T(8,128)(2,1)S(1)}, u32[]{:S(2)}, u32[]{:S(2)}) %collective-permute-start.3) | collective-permute-done | bytes 122912 | tf_op jit(solution)/shard_map/ppermute | solution.py:409
  27.0 3.7 %collective-permute-done.2.qx = bf16[80,768]{1,0:T(8,128)(2,1)S(1)} collective-permute-done((bf16[80,768]{1,0:T(8,128)(2,1)S(1)}, bf16[80,768]{1,0:T(8,128)(2,1)S(1)}, u32[]{:S(2)}, u32[]{:S(2)}) %collective-permute-start.2) | collective-permute-done | bytes 122912 | tf_op jit(solution)/shard_map/ppermute | solution.py:409
  30.8 3.1 %collective-permute-start.5 = (bf16[4,32,1152]{2,1,0:T(8,128)(2,1)S(1)}, bf16[4,32,1152]{2,1,0:T(8,128)(2,1)S(1)}, u32[]{:S(2)}, u32[]{:S(2)}) collective-permute-start(bf16[4,32,1152]{2,1,0:T(8,128)(2,1)S(1)} %get-tuple-element.63), channel_id=1, source_target_pairs={{0,6},{1,7},{2,0},{3,1},{4,2},{5,3},{6,4},{7,5},{8,14},{9,15},{10,... | collective-permute-start | bytes 884744 | tf_op jit(solution)/shard_map/ppermute | solution.py:409
  34.0 10.2 %prepare.1 = (bf16[4,640,768]{2,1,0:T(8,128)(2,1)}, f32[4,640,512]{2,1,0:T(8,128)}, f32[4,640,128]{2,1,0:T(8,128)}, f32[4,640,128]{2,1,0:T(8,128)}, bf16[2048,128]{1,0:T(8,128)(2,1)}, /*index=5*/s32[32]{0:T(128)S(1)}) custom-call(s32[3]{0:T(128)S(1)} %copy-done, s32[8,64]{1,0:T(8,128)S(1)} %copy-done.1, s32[2,8]{1,0:T(2,128)S(1)} %bitcast.32, ...), custom_call_target="tpu_custom_call" | custom-call | flops 3000000000 | bytes 14000000 | tf_op jit(solution)/shard_map/prepare/pallas_call | solution.py:423
  46.4 17.8 %attend.1 = (bf16[96,512]{1,0:T(8,128)(2,1)S(1)}, bf16[80,512]{1,0:T(8,128)(2,1)S(1)}, bf16[176,512]{1,0:T(8,128)(2,1)S(1)}, bf16[176,512]{1,0:T(8,128)(2,1)S(1)}, bf16[176,512]{1,0:T(8,128)(2,1)S(1)}) custom-call(s32[3]{0:T(128)S(1)} %copy-done, s32[32]{0:T(128)S(1)} %get-tuple-element.37.table, bf16[4,640,768]{2,1,0:T(8,128)(2,1)} %get-tuple-element.38.q_ref, ...), custom_call_target="tpu_custom_call" | custom-call | flops 12000000000 | bytes 15000000 | tf_op jit(solution)/shard_map/attend/pallas_call | solution.py:467
  64.1 2.5 %collective-permute-start.9 = (bf16[176,512]{1,0:T(8,128)(2,1)S(1)}, bf16[176,512]{1,0:T(8,128)(2,1)S(1)}, u32[]{:S(2)}, u32[]{:S(2)}) collective-permute-start(bf16[176,512]{1,0:T(8,128)(2,1)S(1)} %get-tuple-element.47), channel_id=1, source_target_pairs={{0,8},{8,16},{16,24},{24,0},{1,9},{9,17},{17,25},{25,1},{2,10},{10... | collective-permute-start | bytes 540680 | tf_op jit(solution)/shard_map/ppermute | solution.py:409
  68.0 1.9 %collective-permute-start.12 = (bf16[80,512]{1,0:T(8,128)(2,1)S(1)}, bf16[80,512]{1,0:T(8,128)(2,1)S(1)}, u32[]{:S(2)}, u32[]{:S(2)}) collective-permute-start(bf16[80,512]{1,0:T(8,128)(2,1)S(1)} %get-tuple-element.50), channel_id=1, source_target_pairs={{0,24},{8,0},{16,8},{24,16},{1,25},{9,1},{17,9},{25,17},{2,26},{10... | collective-permute-start | bytes 245768 | tf_op jit(solution)/shard_map/ppermute | solution.py:409
  70.8 5.1 %collective-permute-done.12 = bf16[80,512]{1,0:T(8,128)(2,1)S(1)} collective-permute-done((bf16[80,512]{1,0:T(8,128)(2,1)S(1)}, bf16[80,512]{1,0:T(8,128)(2,1)S(1)}, u32[]{:S(2)}, u32[]{:S(2)}) %collective-permute-start.12) | collective-permute-done | bytes 81952 | tf_op jit(solution)/shard_map/ppermute | solution.py:409
  75.8 2.7 %collective-permute-start.13 = (bf16[80,512]{1,0:T(8,128)(2,1)S(1)}, bf16[80,512]{1,0:T(8,128)(2,1)S(1)}, u32[]{:S(2)}, u32[]{:S(2)}) collective-permute-start(bf16[80,512]{1,0:T(8,128)(2,1)S(1)} %collective-permute-done.12), channel_id=1, source_target_pairs={{0,24},{8,0},{16,8},{24,16},{1,25},{9,1},{17,9},{25,17},{2,26},{10... | collective-permute-start | bytes 245768 | tf_op jit(solution)/shard_map/ppermute | solution.py:409
  78.5 2.1 %collective-permute-done.13.g4 = bf16[80,512]{1,0:T(8,128)(2,1)S(1)} collective-permute-done((bf16[80,512]{1,0:T(8,128)(2,1)S(1)}, bf16[80,512]{1,0:T(8,128)(2,1)S(1)}, u32[]{:S(2)}, u32[]{:S(2)}) %collective-permute-start.13) | collective-permute-done | bytes 81952 | tf_op jit(solution)/shard_map/ppermute | solution.py:409
  80.6 2.4 %merge_project.1 = (bf16[160,512]{1,0:T(8,128)(2,1)S(1)}, bf16[160,896]{1,0:T(8,128)(2,1)S(1)}, bf16[160,896]{1,0:T(8,128)(2,1)S(1)}) custom-call(s32[3]{0:T(128)S(1)} %copy-done, bf16[176,512]{1,0:T(8,128)(2,1)S(1)} %get-tuple-element.46.g0, bf16[176,512]{1,0:T(8,128)(2,1)S(1)} %collective-permute-done.9.g1, ...), custom_call_target="tpu_custom_call" | custom-call | tf_op jit(solution)/shard_map/merge_project/pallas_call | solution.py:570
  83.1 1.6 %collective-permute-done.14 = bf16[160,896]{1,0:T(8,128)(2,1)S(1)} collective-permute-done((bf16[160,896]{1,0:T(8,128)(2,1)S(1)}, bf16[160,896]{1,0:T(8,128)(2,1)S(1)}, u32[]{:S(2)}, u32[]{:S(2)}) %collective-permute-start.14) | collective-permute-done | bytes 286752 | tf_op jit(solution)/shard_map/ppermute | solution.py:413
  84.8 2.0 %project_away.1 = bf16[3,160,896]{2,1,0:T(8,128)(2,1)S(1)} custom-call(s32[3]{0:T(128)S(1)} %copy-done, bf16[160,512]{1,0:T(8,128)(2,1)S(1)} %get-tuple-element.54.head_ref, bf16[512,7168]{1,0:T(8,128)(2,1)S(1)} %bitcast.30), custom_call_target="tpu_custom_call" | custom-call | flops 1000000000 | bytes 4000000 | tf_op jit(solution)/shard_map/project_away/pallas_call | solution.py:494
  87.2 3.0 %collective-permute-start.18 = (bf16[80,896]{1,0:T(8,128)(2,1)S(1)}, bf16[80,896]{1,0:T(8,128)(2,1)S(1)}, u32[]{:S(2)}, u32[]{:S(2)}) collective-permute-start(bf16[80,896]{1,0:T(8,128)(2,1)S(1)} %get-tuple-element.56), channel_id=1, source_target_pairs={{0,6},{1,7},{2,0},{3,1},{4,2},{5,3},{6,4},{7,5},{8,14},{9,15},{10,... | collective-permute-start | bytes 430088 | tf_op jit(solution)/shard_map/ppermute | solution.py:409
  90.3 2.0 %project_home.1 = bf16[3,160,896]{2,1,0:T(8,128)(2,1)S(1)} custom-call(s32[3]{0:T(128)S(1)} %copy-done, bf16[160,512]{1,0:T(8,128)(2,1)S(1)} %get-tuple-element.54.head_ref, bf16[512,7168]{1,0:T(8,128)(2,1)S(1)} %bitcast.30), custom_call_target="tpu_custom_call" | custom-call | flops 1000000000 | bytes 4000000 | tf_op jit(solution)/shard_map/project_home/pallas_call | solution.py:494
  92.5 1.7 %collective-permute-done.16 = bf16[80,896]{1,0:T(8,128)(2,1)S(1)} collective-permute-done((bf16[80,896]{1,0:T(8,128)(2,1)S(1)}, bf16[80,896]{1,0:T(8,128)(2,1)S(1)}, u32[]{:S(2)}, u32[]{:S(2)}) %collective-permute-start.16) | collective-permute-done | bytes 143392 | tf_op jit(solution)/shard_map/ppermute | solution.py:409
  94.4 3.0 %collective-permute-start.19 = (bf16[160,896]{1,0:T(8,128)(2,1)S(1)}, bf16[160,896]{1,0:T(8,128)(2,1)S(1)}, u32[]{:S(2)}, u32[]{:S(2)}) collective-permute-start(bf16[160,896]{1,0:T(8,128)(2,1)S(1)} %pad_maximum_fusion.1), channel_id=1, source_target_pairs={{0,6},{1,7},{2,0},{3,1},{4,2},{5,3},{6,4},{7,5},{8,14},{9,15},{10,... | collective-permute-start | bytes 860168 | tf_op jit(solution)/shard_map/ppermute | solution.py:409
  97.5 5.4 %collective-permute-done.19 = bf16[160,896]{1,0:T(8,128)(2,1)S(1)} collective-permute-done((bf16[160,896]{1,0:T(8,128)(2,1)S(1)}, bf16[160,896]{1,0:T(8,128)(2,1)S(1)}, u32[]{:S(2)}, u32[]{:S(2)}) %collective-permute-start.19) | collective-permute-done | bytes 286752 | tf_op jit(solution)/shard_map/ppermute | solution.py:409
  102.9 3.5 %collective-permute-done.17 = bf16[160,896]{1,0:T(8,128)(2,1)S(1)} collective-permute-done((bf16[160,896]{1,0:T(8,128)(2,1)S(1)}, bf16[160,896]{1,0:T(8,128)(2,1)S(1)}, u32[]{:S(2)}, u32[]{:S(2)}) %collective-permute-start.17) | collective-permute-done | bytes 286752 | tf_op jit(solution)/shard_map/ppermute | solution.py:409
  (57 shorter events, 7.0 us)
Async XLA Ops:
  4.4 29.5 %copy-start.3 = (bf16[4,128,512]{2,1,0:T(8,128)(2,1)S(1)}, bf16[4,128,512]{2,1,0:T(8,128)(2,1)}, u32[]{:S(2)}) copy-start(bf16[4,128,512]{2,1,0:T(8,128)(2,1)} %ka_ref.1) | copy-start | bytes 1572868
  4.5 26.3 %all-to-all-start = ((bf16[8,32,1152]{2,1,0:T(8,128)(2,1)}), bf16[8,32,1152]{2,1,0:T(8,128)(2,1)S(1)}, u32[]{:S(2)}, u32[]{:S(2)}) async-start(bf16[8,32,1152]{2,1,0:T(8,128)(2,1)} %get-tuple-element.32), calls=%async_computation | async-start | bytes 1179648 | tf_op jit(solution)/shard_map/all_to_all | solution.py:549
  13.2 7.7 %collective-permute-start.1 = (bf16[160,768]{1,0:T(8,128)(2,1)}, bf16[160,768]{1,0:T(8,128)(2,1)S(1)}, u32[]{:S(2)}, u32[]{:S(2)}) collective-permute-start(bf16[160,768]{1,0:T(8,128)(2,1)} %get-tuple-element.31.q0), channel_id=1, source_target_pairs={{0,24},{8,0},{16,8},{24,16},{1,25},{9,1},{17,9},{25,17},{2,26},{10... | collective-permute-start | bytes 737288 | tf_op jit(solution)/shard_map/ppermute | solution.py:409
  15.9 8.6 %collective-permute-start = (bf16[160,768]{1,0:T(8,128)(2,1)}, bf16[160,768]{1,0:T(8,128)(2,1)S(1)}, u32[]{:S(2)}, u32[]{:S(2)}) collective-permute-start(bf16[160,768]{1,0:T(8,128)(2,1)} %get-tuple-element.31.q0), channel_id=1, source_target_pairs={{0,8},{8,16},{16,24},{24,0},{1,9},{9,17},{17,25},{25,1},{2,10},{10... | collective-permute-start | bytes 737288 | tf_op jit(solution)/shard_map/ppermute | solution.py:409
  20.9 6.1 %collective-permute-start.3 = (bf16[80,768]{1,0:T(8,128)(2,1)S(1)}, bf16[80,768]{1,0:T(8,128)(2,1)S(1)}, u32[]{:S(2)}, u32[]{:S(2)}) collective-permute-start(bf16[80,768]{1,0:T(8,128)(2,1)S(1)} %slice.49), channel_id=1, source_target_pairs={{0,24},{8,0},{16,8},{24,16},{1,25},{9,1},{17,9},{25,17},{2,26},{10... | collective-permute-start | bytes 368648 | tf_op jit(solution)/shard_map/ppermute | solution.py:409
  24.6 6.2 %collective-permute-start.2 = (bf16[80,768]{1,0:T(8,128)(2,1)S(1)}, bf16[80,768]{1,0:T(8,128)(2,1)S(1)}, u32[]{:S(2)}, u32[]{:S(2)}) collective-permute-start(bf16[80,768]{1,0:T(8,128)(2,1)S(1)} %slice.48), channel_id=1, source_target_pairs={{0,8},{8,16},{16,24},{24,0},{1,9},{9,17},{17,25},{25,1},{2,10},{10... | collective-permute-start | bytes 368648 | tf_op jit(solution)/shard_map/ppermute | solution.py:409
  30.8 13.5 %collective-permute-start.6 = (bf16[8,32,1152]{2,1,0:T(8,128)(2,1)S(1)}, bf16[8,32,1152]{2,1,0:T(8,128)(2,1)S(1)}, u32[]{:S(2)}, u32[]{:S(2)}) collective-permute-start(bf16[8,32,1152]{2,1,0:T(8,128)(2,1)S(1)} %all-to-all-done.a0), channel_id=1, source_target_pairs={{0,1},{1,0},{2,3},{3,2},{4,5},{5,4},{6,7},{7,6},{8,9},{9,8},{10,11... | collective-permute-start | bytes 1769480 | tf_op jit(solution)/shard_map/ppermute | solution.py:413
  30.8 13.4 %collective-permute-start.5 = (bf16[4,32,1152]{2,1,0:T(8,128)(2,1)S(1)}, bf16[4,32,1152]{2,1,0:T(8,128)(2,1)S(1)}, u32[]{:S(2)}, u32[]{:S(2)}) collective-permute-start(bf16[4,32,1152]{2,1,0:T(8,128)(2,1)S(1)} %get-tuple-element.63), channel_id=1, source_target_pairs={{0,6},{1,7},{2,0},{3,1},{4,2},{5,3},{6,4},{7,5},{8,14},{9,15},{10,... | collective-permute-start | bytes 884744 | tf_op jit(solution)/shard_map/ppermute | solution.py:409
  33.9 10.3 %collective-permute-start.4 = (bf16[4,32,1152]{2,1,0:T(8,128)(2,1)S(1)}, bf16[4,32,1152]{2,1,0:T(8,128)(2,1)S(1)}, u32[]{:S(2)}, u32[]{:S(2)}) collective-permute-start(bf16[4,32,1152]{2,1,0:T(8,128)(2,1)S(1)} %get-tuple-element.64), channel_id=1, source_target_pairs={{0,2},{1,3},{2,4},{3,5},{4,6},{5,7},{6,0},{7,1},{8,10},{9,11},{10,... | collective-permute-start | bytes 884744 | tf_op jit(solution)/shard_map/ppermute | solution.py:409
  44.3 1.7 %collective-permute-start.7 = (bf16[4,32,1152]{2,1,0:T(8,128)(2,1)S(1)}, bf16[4,32,1152]{2,1,0:T(8,128)(2,1)S(1)}, u32[]{:S(2)}, u32[]{:S(2)}) collective-permute-start(bf16[4,32,1152]{2,1,0:T(8,128)(2,1)S(1)} %collective-permute-done.4.am), channel_id=1, source_target_pairs={{0,1},{1,0},{2,3},{3,2},{4,5},{5,4},{6,7},{7,6},{8,9},{9,8},{10,11... | collective-permute-start | bytes 884744 | tf_op jit(solution)/shard_map/ppermute | solution.py:413
  44.6 1.8 %collective-permute-start.8 = (bf16[4,32,1152]{2,1,0:T(8,128)(2,1)S(1)}, bf16[4,32,1152]{2,1,0:T(8,128)(2,1)S(1)}, u32[]{:S(2)}, u32[]{:S(2)}) collective-permute-start(bf16[4,32,1152]{2,1,0:T(8,128)(2,1)S(1)} %collective-permute-done.5.ap), channel_id=1, source_target_pairs={{0,1},{1,0},{2,3},{3,2},{4,5},{5,4},{6,7},{7,6},{8,9},{9,8},{10,11... | collective-permute-start | bytes 884744 | tf_op jit(solution)/shard_map/ppermute | solution.py:413
  46.4 34.3 %slice-start = ((s8[7340032]{0:T(1024)(128)(4,1)}), s8[4194304]{0:T(1024)(128)(4,1)S(1)}, s32[]{:S(2)}) async-start(s8[7340032]{0:T(1024)(128)(4,1)} %bitcast.29), calls=%async_computation.1 | async-start | bytes 8388608
  46.4 34.3 %slice-start.1 = ((s8[7340032]{0:T(1024)(128)(4,1)}), s8[3145728]{0:T(1024)(128)(4,1)S(1)}, s32[]{:S(2)}) async-start(s8[7340032]{0:T(1024)(128)(4,1)} %bitcast.29), calls=%async_computation.2 | async-start | bytes 6291456
  64.1 16.5 %collective-permute-start.9 = (bf16[176,512]{1,0:T(8,128)(2,1)S(1)}, bf16[176,512]{1,0:T(8,128)(2,1)S(1)}, u32[]{:S(2)}, u32[]{:S(2)}) collective-permute-start(bf16[176,512]{1,0:T(8,128)(2,1)S(1)} %get-tuple-element.47), channel_id=1, source_target_pairs={{0,8},{8,16},{16,24},{24,0},{1,9},{9,17},{17,25},{25,1},{2,10},{10... | collective-permute-start | bytes 540680 | tf_op jit(solution)/shard_map/ppermute | solution.py:409
  66.7 13.9 %collective-permute-start.10 = (bf16[176,512]{1,0:T(8,128)(2,1)S(1)}, bf16[176,512]{1,0:T(8,128)(2,1)S(1)}, u32[]{:S(2)}, u32[]{:S(2)}) collective-permute-start(bf16[176,512]{1,0:T(8,128)(2,1)S(1)} %get-tuple-element.48), channel_id=1, source_target_pairs={{0,24},{8,0},{16,8},{24,16},{1,25},{9,1},{17,9},{25,17},{2,26},{10... | collective-permute-start | bytes 540680 | tf_op jit(solution)/shard_map/ppermute | solution.py:409
  68.0 7.9 %collective-permute-start.12 = (bf16[80,512]{1,0:T(8,128)(2,1)S(1)}, bf16[80,512]{1,0:T(8,128)(2,1)S(1)}, u32[]{:S(2)}, u32[]{:S(2)}) collective-permute-start(bf16[80,512]{1,0:T(8,128)(2,1)S(1)} %get-tuple-element.50), channel_id=1, source_target_pairs={{0,24},{8,0},{16,8},{24,16},{1,25},{9,1},{17,9},{25,17},{2,26},{10... | collective-permute-start | bytes 245768 | tf_op jit(solution)/shard_map/ppermute | solution.py:409
  69.9 8.6 %collective-permute-start.11 = (bf16[96,512]{1,0:T(8,128)(2,1)S(1)}, bf16[96,512]{1,0:T(8,128)(2,1)S(1)}, u32[]{:S(2)}, u32[]{:S(2)}) collective-permute-start(bf16[96,512]{1,0:T(8,128)(2,1)S(1)} %get-tuple-element.49), channel_id=1, source_target_pairs={{0,16},{8,24},{16,0},{24,8},{1,17},{9,25},{17,1},{25,9},{2,18},{10... | collective-permute-start | bytes 294920 | tf_op jit(solution)/shard_map/ppermute | solution.py:409
  75.8 4.8 %collective-permute-start.13 = (bf16[80,512]{1,0:T(8,128)(2,1)S(1)}, bf16[80,512]{1,0:T(8,128)(2,1)S(1)}, u32[]{:S(2)}, u32[]{:S(2)}) collective-permute-start(bf16[80,512]{1,0:T(8,128)(2,1)S(1)} %collective-permute-done.12), channel_id=1, source_target_pairs={{0,24},{8,0},{16,8},{24,16},{1,25},{9,1},{17,9},{25,17},{2,26},{10... | collective-permute-start | bytes 245768 | tf_op jit(solution)/shard_map/ppermute | solution.py:409
  83.0 1.7 %collective-permute-start.14 = (bf16[160,896]{1,0:T(8,128)(2,1)S(1)}, bf16[160,896]{1,0:T(8,128)(2,1)S(1)}, u32[]{:S(2)}, u32[]{:S(2)}) collective-permute-start(bf16[160,896]{1,0:T(8,128)(2,1)S(1)} %get-tuple-element.53), channel_id=1, source_target_pairs={{0,1},{1,0},{2,3},{3,2},{4,5},{5,4},{6,7},{7,6},{8,9},{9,8},{10,11... | collective-permute-start | bytes 860168 | tf_op jit(solution)/shard_map/ppermute | solution.py:413
  86.8 5.5 %collective-permute-start.15 = (bf16[3,160,896]{2,1,0:T(8,128)(2,1)S(1)}, bf16[3,160,896]{2,1,0:T(8,128)(2,1)S(1)}, u32[]{:S(2)}, u32[]{:S(2)}) collective-permute-start(bf16[3,160,896]{2,1,0:T(8,128)(2,1)S(1)} %project_away.1), channel_id=1, source_target_pairs={{0,1},{1,0},{2,3},{3,2},{4,5},{5,4},{6,7},{7,6},{8,9},{9,8},{10,11... | collective-permute-start | bytes 2580488 | tf_op jit(solution)/shard_map/ppermute | solution.py:413
  87.0 7.2 %collective-permute-start.16 = (bf16[80,896]{1,0:T(8,128)(2,1)S(1)}, bf16[80,896]{1,0:T(8,128)(2,1)S(1)}, u32[]{:S(2)}, u32[]{:S(2)}) collective-permute-start(bf16[80,896]{1,0:T(8,128)(2,1)S(1)} %get-tuple-element.55), channel_id=1, source_target_pairs={{0,2},{1,3},{2,4},{3,5},{4,6},{5,7},{6,0},{7,1},{8,10},{9,11},{10,... | collective-permute-start | bytes 430088 | tf_op jit(solution)/shard_map/ppermute | solution.py:409
  87.2 7.0 %collective-permute-start.18 = (bf16[80,896]{1,0:T(8,128)(2,1)S(1)}, bf16[80,896]{1,0:T(8,128)(2,1)S(1)}, u32[]{:S(2)}, u32[]{:S(2)}) collective-permute-start(bf16[80,896]{1,0:T(8,128)(2,1)S(1)} %get-tuple-element.56), channel_id=1, source_target_pairs={{0,6},{1,7},{2,0},{3,1},{4,2},{5,3},{6,4},{7,5},{8,14},{9,15},{10,... | collective-permute-start | bytes 430088 | tf_op jit(solution)/shard_map/ppermute | solution.py:409
  94.4 8.5 %collective-permute-start.19 = (bf16[160,896]{1,0:T(8,128)(2,1)S(1)}, bf16[160,896]{1,0:T(8,128)(2,1)S(1)}, u32[]{:S(2)}, u32[]{:S(2)}) collective-permute-start(bf16[160,896]{1,0:T(8,128)(2,1)S(1)} %pad_maximum_fusion.1), channel_id=1, source_target_pairs={{0,6},{1,7},{2,0},{3,1},{4,2},{5,3},{6,4},{7,5},{8,14},{9,15},{10,... | collective-permute-start | bytes 860168 | tf_op jit(solution)/shard_map/ppermute | solution.py:409
  97.4 9.0 %collective-permute-start.17 = (bf16[160,896]{1,0:T(8,128)(2,1)S(1)}, bf16[160,896]{1,0:T(8,128)(2,1)S(1)}, u32[]{:S(2)}, u32[]{:S(2)}) collective-permute-start(bf16[160,896]{1,0:T(8,128)(2,1)S(1)} %pad_maximum_fusion), channel_id=1, source_target_pairs={{0,2},{1,3},{2,4},{3,5},{4,6},{5,7},{6,0},{7,1},{8,10},{9,11},{10,... | collective-permute-start | bytes 860168 | tf_op jit(solution)/shard_map/ppermute | solution.py:409
  (7 other events, 189.5 us)
where the time goes:
time: 109 us; the launch traced here: 107 us
  Pallas kernels  38.1 us (35%)
  starting transfers between devices  34.9 us (32%)
  waiting for transfers between devices  31.9 us (29%)
  other arithmetic  1.88 us (2%)
    ppermute x15, waiting for transfers between devices, shift(): lax.ppermute(value, axis, [(i, (i + by) % size) for i in range(size)])  28.9 us
    ppermute x15, starting transfers between devices, shift(): lax.ppermute(value, axis, [(i, (i + by) % size) for i in range(size)])  25.3 us
    pallas_call x1, Pallas kernels, attend(): pl.pallas_call(attend_kernel, grid_spec=pltpu.PrefetchScalarGridSpec(num_...  17.8 us
    pallas_call x1, Pallas kernels, prepare(): pl.pallas_call(ready_kernel, grid_spec=pltpu.PrefetchScalarGridSpec(num_s...  10.2 us
    all_to_all x1, starting transfers between devices, local(): a0 = lax.all_to_all(picked, 'pool', split_axis=0, concat_axis=0, tiled=True)  8.71 us
    pallas_call x2, Pallas kernels, rest(): pl.pallas_call(partial(rest_kernel, other), grid_spec=pltpu.PrefetchScala...  4.01 us
    pallas_call x1, Pallas kernels, local(): pl.pallas_call(pick_kernel, grid_spec=pltpu.PrefetchScalarGridSpec(num_sc...  3.75 us
    ppermute x5, waiting for transfers between devices, swap_core(): return lax.ppermute(value, 'head', [(i, i ^ 1) for i in range(8)])  3.05 us
  transfers between devices with their start and end apart: 21, of which 11 were waited for; matrix products, arithmetic and copies ran while one was open for 0% of the time, Pallas kernels for 11%

commit v1 on v0

--- a/solution.py
+++ b/solution.py
@@ -18,7 +18,6 @@
 TOK = 160
 SLOTS = 16
 KEYS = SLOTS * BLK
-CUT = 96
 KW = 768
 BIG = 2.0**100
 SCALE = (QK_NOPE + ROPE) ** (-0.5)
@@ -108,74 +107,79 @@
     )
 
 
-def ready_kernel(
-    ids, holder, prior, counts,
-    q0, qm, qp, qx, qy, ka_ref, nl_ref,
-    q_out, acc_out, mx_out, sm_out, mark_out, table,
-    part, kn, seen,
-):
+def mark(n, base, keys0, keys1):
+    row = iota((n, 128), 0) + base
+    lane = iota((n, 128), 1)
+    miss0 = (lane == 0) & jnp.logical_not(keys0(row))
+    miss1 = (lane == 1) & jnp.logical_not(keys1(row))
+    return jnp.where(miss0 | miss1, -BIG, 0.0).astype(BF)
+
+
+def plan(ids, holder, prior, counts, mark_out, table, seen):
+    group = ids[0]
+    for i in range(SLOTS):
+        table[i] = -1
+    for i in range(8):
+        seen[i] = 0
+    own = prior[0, group]
+    total = own + prior[1, group]
+
+    def entry(e, carry):
+        filled, mine = carry
+        where = holder[group, e]
+        hit = (where & 3) == ids[1]
+        p = where >> 2
+
+        @pl.when(hit)
+        def _():
+            s = seen[p]
+            seen[p] = s + 1
+            table[p * 2 + s] = filled
+
+        add = hit.astype(jnp.int32)
+        return filled + add, mine + jnp.where(e < own, add, 0)
+
+    filled, mine = lax.fori_loop(0, total, entry, (jnp.int32(0), jnp.int32(0)))
+    end0 = mine * BLK
+    end1 = filled * BLK
+    table[SLOTS] = end0
+    table[SLOTS + 1] = end1
+    table[SLOTS + 2] = counts[0, group]
+    for i in range(SLOTS + 3, 32):
+        table[i] = 0
+    for i in range(SLOTS):
+        dead = table[i] < 0
+
+        @pl.when(dead)
+        def _():
+            table[i] = filled
+
+        filled = filled + dead.astype(jnp.int32)
+
+    def marks(i, _):
+        at = pl.multiple_of(i * BLK, BLK)
+        mark_out[pl.ds(at, BLK), :] = mark(
+            BLK, at, lambda r: r < end0, lambda r: (r >= end0) & (r < end1)
+        )
+        return 0
+
+    lax.fori_loop(0, SLOTS, marks, 0)
+
+
+def ready_kernel(own, ids, holder, prior, counts, *refs):
+    if own:
+        q0, ka_ref, nl_ref, q_out, acc_out, mx_out, sm_out, mark_out, table, part, kn, seen = refs
+    else:
+        qm, qp, qx, qy, ka_ref, nl_ref = refs[:6]
+        q_out, acc_out, mx_out, sm_out, part, kn = refs[10:]
     step = pl.program_id(0)
-    group = ids[0]
     ctx = ids[1]
-    n0 = counts[0, group]
-
-    def mark(n, base, keys0, keys1):
-        row = iota((n, 128), 0) + base
-        lane = iota((n, 128), 1)
-        miss0 = (lane == 0) & jnp.logical_not(keys0(row))
-        miss1 = (lane == 1) & jnp.logical_not(keys1(row))
-        return jnp.where(miss0 | miss1, -BIG, 0.0).astype(BF)
+    n0 = counts[0, ids[0]]
 
     @pl.when(step == 0)
     def _():
-        for i in range(SLOTS):
-            table[i] = -1
-        for i in range(8):
-            seen[i] = 0
-        own = prior[0, group]
-        total = own + prior[1, group]
-
-        def entry(e, carry):
-            filled, mine = carry
-            where = holder[group, e]
-            hit = (where & 3) == ctx
-            p = where >> 2
-
-            @pl.when(hit)
-            def _():
-                s = seen[p]
-                seen[p] = s + 1
-                table[p * 2 + s] = filled
-
-            add = hit.astype(jnp.int32)
-            return filled + add, mine + jnp.where(e < own, add, 0)
-
-        filled, mine = lax.fori_loop(0, total, entry, (jnp.int32(0), jnp.int32(0)))
-        end0 = mine * BLK
-        end1 = filled * BLK
-        table[SLOTS] = end0
-        table[SLOTS + 1] = end1
-        table[SLOTS + 2] = n0
-        for i in range(SLOTS + 3, 32):
-            table[i] = 0
-        for i in range(SLOTS):
-            dead = table[i] < 0
-
-            @pl.when(dead)
-            def _():
-                table[i] = filled
-
-            filled = filled + dead.astype(jnp.int32)
-
-        def marks(i, _):
-            at = pl.multiple_of(i * BLK, BLK)
-            mark_out[pl.ds(at, BLK), :] = mark(
-                BLK, at, lambda r: r < end0, lambda r: (r >= end0) & (r < end1)
-            )
-            return 0
-
-        lax.fori_loop(0, SLOTS, marks, 0)
-
+        if own:
+            plan(ids, holder, prior, counts, mark_out, table, seen)
         even, odd, rope = align(nl_ref[...])
         rope = both_ropes(rope)
         kn[...] = jnp.zeros(kn.shape, BF)
@@ -191,20 +195,19 @@
         kn[:, 640:768] = mark(
             256, 0, lambda r: new_position(r) < n0, lambda r: new_position(r) >= n0
         )
+
+    if own:
         part[...] = q0[...]
-
-    @pl.when(step == 1)
-    def _():
-        part[...] = qm[...]
-
-    @pl.when(step == 2)
-    def _():
-        part[...] = qp[...]
-
-    @pl.when(step == 3)
-    def _():
-        part[0:80] = qx[...]
-        part[80:160] = qy[...]
+    else:
+        for i, pieces in enumerate(((qm,), (qp,), (qx, qy))):
+
+            @pl.when(step == i)
+            def _():
+                n = TOK // len(pieces)
+                for k, piece in enumerate(pieces):
+                    part[k * n : (k + 1) * n] = piece[...]
+
+        step = step + 1
 
     rows = HEADS * TOK
     t0 = ((ctx + turn_of(step)) & 3) * TOK
@@ -250,7 +253,7 @@
 def attend_kernel(
     ids, table,
     q_ref, acc0, mx0, sm0, va_ref, mark_ref, a0, am, ap, b0, bm, bp,
-    far_a, far_b, low_ref, high_ref, kept_ref,
+    out_ref,
     kc, kb, acc, mx, sm, sem,
 ):
     step = pl.program_id(0)
@@ -334,32 +337,16 @@
             for i, value in enumerate((one, two, three)):
                 stats = jnp.where(lane16 == base + i, value[cut], stats)
 
-    def emit(out_ref, first, count):
-        for j in range(HEADS):
-            out_ref[0:count, j * 128 : (j + 1) * 128] = heads[j][first : first + count]
-        if first + count == TOK:
-            out_ref[count : count + STAT, 0:128] = stats.astype(BF)
-            out_ref[count : count + STAT, 128:512] = jnp.zeros((STAT, 384), BF)
-
-    for turn, parts in (
-        (0, ((kept_ref, 0, TOK),)),
-        (1, ((high_ref, 0, TOK),)),
-        (2, ((far_a, 0, CUT), (far_b, CUT, TOK - CUT))),
-        (3, ((low_ref, 0, TOK),)),
-    ):
-
-        @pl.when(step == ORDER.index(turn))
-        def _():
-            for part in parts:
-                emit(*part)
-
-
-def merge(kept, low, high, far_a, far_b):
+    for j in range(HEADS):
+        out_ref[0, 0:TOK, j * 128 : (j + 1) * 128] = heads[j]
+    out_ref[0, TOK : TOK + STAT, 0:128] = stats.astype(BF)
+    out_ref[0, TOK : TOK + STAT, 128:512] = jnp.zeros((STAT, 384), BF)
+
+
+def merge_kernel(got_ref, head_ref):
     lane_in = iota((128, 512), 0)
     lane_head = iota((128, 512), 1) // 128
-    outs = []
-    tails = [ref[TOK : TOK + STAT, 0:128] for ref in (kept, low, high)]
-    stats = jnp.concatenate([*tails, far_b[TOK - CUT : TOK - CUT + STAT, 0:128]], axis=0)
+    stats = jnp.concatenate([got_ref[c, TOK : TOK + STAT, 0:128] for c in range(4)], axis=0)
     for k in range(TOK // 16):
         pickup = ((lane_in >= 12 * k + 3 * lane_head) & (lane_in < 12 * k + 3 * lane_head + 3))
         lse = jnp.dot(stats, pickup.astype(BF), preferred_element_type=F32)
@@ -368,41 +355,21 @@
         weight = [jnp.exp(v - top) for v in lse]
         total = weight[0] + weight[1] + weight[2] + weight[3]
         at = slice(k * 16, (k + 1) * 16)
-        far = far_a[at, :] if k * 16 < CUT else far_b[k * 16 - CUT : k * 16 - CUT + 16, :]
-        values = (kept[at, :], low[at, :], high[at, :], far)
-        mixed = sum(w * v.astype(F32) for w, v in zip(weight, values))
-        outs.append((mixed / total).astype(BF))
-    return outs
-
-
-def fetch(ids, w_ref, held, sem, picks):
-    copies = []
-    for i, (turn, other) in enumerate(picks):
-        y = ((ids[2] >> 1) + turn) & 3
-        column = (y * 2 + ((ids[2] & 1) ^ other)) * 896
-        copies.append(
-            pltpu.make_async_copy(
-                w_ref.at[:, pl.ds(pl.multiple_of(column, 128), 896)], held.at[i], sem.at[i]
-            )
-        )
-        copies[-1].start()
-    return copies
-
-
-def first_kernel(ids, g0, g1, g2, g3, g4, w_ref, head_ref, away_ref, home_ref, held, sem):
-    copies = fetch(ids, w_ref, held, sem, ((2, 1), (2, 0)))
-    for k, value in enumerate(merge(g0, g1, g2, g3, g4)):
-        head_ref[k * 16 : (k + 1) * 16, :] = value
-    for i, out in enumerate((away_ref, home_ref)):
-        copies[i].wait()
-        out[...] = jnp.dot(head_ref[...], held[i], preferred_element_type=F32).astype(BF)
-
-
-def rest_kernel(other, ids, head_ref, w_ref, out_ref, held, sem):
-    copies = fetch(ids, w_ref, held, sem, ((1, other), (3, other), (0, other)))
-    for i in range(3):
-        copies[i].wait()
-        out_ref[i] = jnp.dot(head_ref[...], held[i], preferred_element_type=F32).astype(BF)
+        mixed = sum(w * got_ref[c, at, :].astype(F32) for c, w in enumerate(weight))
+        head_ref[at, :] = (mixed / total).astype(BF)
+
+
+def project_kernel(ids, head_ref, other_ref, w_ref, x_ref, out_ref):
+    core = ids[2] & 1
+    for y in range(4):
+        column = pl.multiple_of((2 * y + core) * 896, 128)
+        total = jnp.dot(
+            head_ref[...], w_ref[:, pl.ds(column, 896)], preferred_element_type=F32
+        )
+        total += jnp.dot(
+            other_ref[...], x_ref[:, y * 896 : (y + 1) * 896], preferred_element_type=F32
+        )
+        out_ref[y] = total.astype(BF)
 
 
 def shift(value, axis, by, size):
@@ -417,44 +384,44 @@
     return pl.BlockSpec(shape, lambda i, *_: (0,) * len(shape))
 
 
-def prepare(ids, hit_holder, prior_blocks, new_counts, queries, key_absorb, new_latent):
+def prepare(ids, hit_holder, prior, counts, queries, key_absorb, new_latent, before=None):
+    own = before is None
     rows = HEADS * TOK
-    tile = lambda n: pl.BlockSpec((1, rows, n), lambda i, *_: (i, 0, 0))
+    tile = lambda n: pl.BlockSpec((1, rows, n), lambda i, *_: (i + (not own), 0, 0))
+    kept = [((KW, BF), 0), ((512, F32), 1), ((128, F32), 2), ((128, F32), 3)]
+    out_specs = [tile(shape[0]) for shape, _ in kept]
+    out_shape = [pltpu.HBM((4, rows, n), kind) for (n, kind), _ in kept]
+    scratch = [pltpu.VMEM((TOK, 768), BF), pltpu.VMEM((256, KW), BF)]
+    aliases = {}
+    if own:
+        out_specs += [whole(KEYS, 128), pl.BlockSpec(memory_space=pltpu.SMEM)]
+        out_shape += [pltpu.HBM((KEYS, 128), BF), jax.ShapeDtypeStruct((32,), jnp.int32)]
+        scratch += [pltpu.SMEM((8,), jnp.int32)]
+        before = ()
+    else:
+        before = [pltpu.with_memory_space_constraint(value, pltpu.HBM) for value in before]
+        aliases = {4 + len(queries) + 2 + i: i for i in range(4)}
     return pl.pallas_call(
-        ready_kernel,
+        partial(ready_kernel, own),
         grid_spec=pltpu.PrefetchScalarGridSpec(
             num_scalar_prefetch=4,
-            grid=(4,),
-            in_specs=[
-                whole(TOK, 768), whole(TOK, 768), whole(TOK, 768), whole(80, 768), whole(80, 768),
-                whole(HEADS, 128, 512),
-                whole(80, WIDE2),
-            ],
-            out_specs=[
-                tile(KW), tile(512), tile(128), tile(128),
-                whole(KEYS, 128),
-                pl.BlockSpec(memory_space=pltpu.SMEM),
-            ],
-            scratch_shapes=[
-                pltpu.VMEM((TOK, 768), BF),
-                pltpu.VMEM((256, KW), BF),
-                pltpu.SMEM((8,), jnp.int32),
-            ],
-        ),
-        out_shape=[
-            pltpu.HBM((4, rows, KW), BF),
-            pltpu.HBM((4, rows, 512), F32),
-            pltpu.HBM((4, rows, 128), F32),
-            pltpu.HBM((4, rows, 128), F32),
-            pltpu.HBM((KEYS, 128), BF),
-            jax.ShapeDtypeStruct((32,), jnp.int32),
-        ],
+            grid=(1 if own else 3,),
+            in_specs=[whole(*value.shape) for value in queries]
+            + [whole(HEADS, 128, 512), whole(80, WIDE2)]
+            + [pl.BlockSpec(memory_space=pltpu.HBM)] * len(before),
+            out_specs=out_specs,
+            scratch_shapes=scratch,
+        ),
+        out_shape=out_shape,
+        input_output_aliases=aliases,
         compiler_params=pltpu.CompilerParams(vmem_limit_bytes=28 * 2**20),
         cost_estimate=pl.CostEstimate(
-            flops=3 * 10**9, bytes_accessed=14 * 10**6, transcendentals=10**6
-        ),
-        name="prepare",
-    )(ids, hit_holder, prior_blocks, new_counts, *queries, key_absorb, new_latent)
+            flops=10**9 * (1 if own else 3),
+            bytes_accessed=4 * 10**6 * (1 if own else 3),
+            transcendentals=10**6,
+        ),
+        name="prepare_own" if own else "prepare_others",
+    )(ids, hit_holder, prior, counts, *queries, key_absorb, new_latent, *before)
 
 
 def attend(ids, ready, pieces, value_absorb):
@@ -463,7 +430,6 @@
     ]
     rows = HEADS * TOK
     tile = lambda n: pl.BlockSpec((1, rows, n), lambda i, *_: (i, 0, 0))
-    out_rows = (CUT, TOK - CUT + STAT, TOK + STAT, TOK + STAT, TOK + STAT)
     return pl.pallas_call(
         attend_kernel,
         grid_spec=pltpu.PrefetchScalarGridSpec(
@@ -471,7 +437,9 @@
             grid=(4,),
             in_specs=[tile(KW), tile(512), tile(128), tile(128), whole(HEADS, 512, 128)]
             + [pl.BlockSpec(memory_space=pl.ANY)] * 7,
-            out_specs=[whole(n, 512) for n in out_rows],
+            out_specs=pl.BlockSpec(
+                (1, TOK + STAT, 512), lambda i, ids, _: ((ids[1] + turn_of(i)) & 3, 0, 0)
+            ),
             scratch_shapes=[
                 pltpu.VMEM((2, 2, 8, 32, WIDE2), BF),
                 pltpu.VMEM((KEYS, KW), BF),
@@ -481,32 +449,13 @@
                 pltpu.SemaphoreType.DMA((3,)),
             ],
         ),
-        out_shape=[jax.ShapeDtypeStruct((n, 512), BF) for n in out_rows],
+        out_shape=jax.ShapeDtypeStruct((4, TOK + STAT, 512), BF),
         compiler_params=pltpu.CompilerParams(vmem_limit_bytes=40 * 2**20),
         cost_estimate=pl.CostEstimate(
             flops=12 * 10**9, bytes_accessed=15 * 10**6, transcendentals=5 * 10**6
         ),
         name="attend",
     )(ids, ready[5], q_all, acc0, mx0, sm0, value_absorb, marks, *pieces)
-
-
-def rest(other, ids, heads, out_weight):
-    return pl.pallas_call(
-        partial(rest_kernel, other),
-        grid_spec=pltpu.PrefetchScalarGridSpec(
-            num_scalar_prefetch=1,
-            grid=(1,),
-            in_specs=[whole(TOK, 512), pl.BlockSpec(memory_space=pl.ANY)],
-            out_specs=whole(3, TOK, 896),
-            scratch_shapes=[pltpu.VMEM((3, 512, 896), BF), pltpu.SemaphoreType.DMA((3,))],
-        ),
-        out_shape=jax.ShapeDtypeStruct((3, TOK, 896), BF),
-        compiler_params=pltpu.CompilerParams(vmem_limit_bytes=12 * 2**20),
-        cost_estimate=pl.CostEstimate(
-            flops=1 * 10**9, bytes_accessed=4 * 10**6, transcendentals=0
-        ),
-        name="project_home" if other == 0 else "project_away",
-    )(ids, heads, out_weight)
 
 
 def local(
@@ -543,65 +492,63 @@
 
     qm = shift(queries, "ctx", 1, 4)
     qp = shift(queries, "ctx", -1, 4)
+    queries, qm, qp = lax.optimization_barrier((queries, qm, qp))
     qx = shift(qm[:80], "ctx", 1, 4)
     qy = shift(qp[80:], "ctx", -1, 4)
 
     a0 = lax.all_to_all(picked, "pool", split_axis=0, concat_axis=0, tiled=True)
 
-    a0, qx, qy = lax.optimization_barrier((a0, qx, qy))
+    prepared = prepare(
+        ids, hit_holder, prior, counts, (queries,), key_absorb, new_latent
+    )
+    a0, qx, qy, table = lax.optimization_barrier((a0, qx, qy, prepared[5]))
     am = shift(a0[:4], "head", 2, 8)
     ap = shift(a0[4:], "head", -2, 8)
     b0 = swap_core(a0)
     ready = prepare(
-        ids, hit_holder, prior, counts, (queries, qm, qp, qx, qy), key_absorb, new_latent
-    )
-    table, am, ap, b0 = lax.optimization_barrier((ready[5], am, ap, b0))
+        ids, hit_holder, prior, counts, (qm, qp, qx, qy), key_absorb, new_latent, prepared[:4]
+    )
+    queries_ready, am, ap, b0 = lax.optimization_barrier((ready[0], am, ap, b0))
     bm = swap_core(am)
     bp = swap_core(ap)
-    far_a, far_b, to_low, to_high, kept = attend(
-        ids, (*ready[:5], table), (a0, am, ap, b0, bm, bp), value_absorb
-    )
-    far_b = shift(far_b, "ctx", -1, 4)
-    far_a = shift(far_a, "ctx", 2, 4)
-    from_low = shift(to_high, "ctx", 1, 4)
-    from_high = shift(to_low, "ctx", -1, 4)
-    far_b = shift(far_b, "ctx", -1, 4)
-
-    heads, away2, home2 = pl.pallas_call(
-        first_kernel,
+    partial_out = attend(
+        ids,
+        (queries_ready, *ready[1:4], prepared[4], table),
+        (a0, am, ap, b0, bm, bp),
+        value_absorb,
+    )
+    partial_out, late_weight = lax.optimization_barrier((partial_out, out_weight))
+    got = lax.all_to_all(partial_out, "ctx", split_axis=0, concat_axis=0, tiled=True)
+    other_columns = [
+        lax.dynamic_slice(late_weight, (0, (2 * y + 1 - (ids[2] & 1)) * 896), (512, 896))
+        for y in range(4)
+    ]
+    other_weight = swap_core(jnp.concatenate(other_columns, axis=1))
+
+    heads = pl.pallas_call(
+        merge_kernel,
+        out_shape=jax.ShapeDtypeStruct((TOK, 512), BF),
+        compiler_params=pltpu.CompilerParams(vmem_limit_bytes=8 * 2**20),
+        name="merge",
+    )(got)
+    other_heads = swap_core(heads)
+    vmem = pl.BlockSpec(memory_space=pltpu.VMEM)
+    shares = pl.pallas_call(
+        project_kernel,
         grid_spec=pltpu.PrefetchScalarGridSpec(
             num_scalar_prefetch=1,
-            grid=(1,),
-            in_specs=[whole(TOK + STAT, 512)] * 3
-            + [whole(CUT, 512), whole(TOK - CUT + STAT, 512)]
-            + [pl.BlockSpec(memory_space=pl.ANY)],
-            out_specs=[whole(TOK, 512), whole(TOK, 896), whole(TOK, 896)],
-            scratch_shapes=[pltpu.VMEM((2, 512, 896), BF), pltpu.SemaphoreType.DMA((2,))],
-        ),
-        out_shape=[
-            jax.ShapeDtypeStruct((TOK, 512), BF),
-            jax.ShapeDtypeStruct((TOK, 896), BF),
-            jax.ShapeDtypeStruct((TOK, 896), BF),
-        ],
-        compiler_params=pltpu.CompilerParams(vmem_limit_bytes=12 * 2**20),
-        name="merge_project",
-    )(ids, kept, from_low, from_high, far_a, far_b, out_weight)
-    across = swap_core(away2)
-    opposite = home2.astype(F32) + across.astype(F32)
-    part_a = opposite[:80].astype(BF)
-    part_b = opposite[80:].astype(BF)
-    heads, part_a, part_b = lax.optimization_barrier((heads, part_a, part_b))
-    part_a = shift(part_a, "head", 2, 8)
-    part_b = shift(part_b, "head", -2, 8)
-    away = rest(1, ids, heads, out_weight)
-    arrived = swap_core(away)
-    home = rest(0, ids, heads, out_weight)
-    both = home.astype(F32) + arrived.astype(F32)
-    up = jnp.concatenate([both[0, :80] + part_a.astype(F32), both[0, 80:]], axis=0).astype(BF)
-    down = jnp.concatenate([both[1, :80], both[1, 80:] + part_b.astype(F32)], axis=0).astype(BF)
-    got_up = shift(up, "head", 2, 8)
-    got_down = shift(down, "head", -2, 8)
-    return (both[2] + got_up.astype(F32) + got_down.astype(F32)).astype(BF)
+            in_specs=[vmem] * 4,
+            out_specs=vmem,
+        ),
+        out_shape=jax.ShapeDtypeStruct((4, TOK, 896), BF),
+        compiler_params=pltpu.CompilerParams(vmem_limit_bytes=24 * 2**20),
+        name="project",
+    )(ids, heads, other_heads, out_weight, other_weight)
+    shares = lax.all_to_all(
+        shares, "head", split_axis=0, concat_axis=0, tiled=True,
+        axis_index_groups=[[0, 2, 4, 6], [1, 3, 5, 7]],
+    )
+    return jnp.sum(shares.astype(F32), axis=0).astype(BF)
 
 
 def solution(mesh):

time: 109 us -> 115 us (1.055)
  the two profiles are of different devices: /device:TPU:32 before, /device:TPU:64 now
where the time goes in v1:
time: 115 us; the launch traced here: 113 us
  Pallas kernels  38.9 us (34%)
  blocking collectives  34.3 us (30%)
  starting transfers between devices  19.2 us (17%)
  local copies, waits for them, and re-layouts  10.1 us (9%)
  waiting for transfers between devices  8.56 us (7%)
  other arithmetic  1.92 us (2%)
    pallas_call x1, Pallas kernels, attend(): pl.pallas_call(attend_kernel, grid_spec=pltpu.PrefetchScalarGridSpec(num_...  19.6 us
    all_to_all x1, blocking collectives, local(): lax.all_to_all(shares, 'head', split_axis=0, concat_axis=0, tiled=True, a...  19.5 us
    all_to_all x1, blocking collectives, local(): lax.all_to_all(partial_out, 'ctx', split_axis=0, concat_axis=0, tiled=True)  14.8 us
    pallas_call x2, Pallas kernels, prepare(): pl.pallas_call(partial(ready_kernel, own), grid_spec=pltpu.PrefetchScalar...  12.4 us
    ppermute x6, starting transfers between devices, shift(): lax.ppermute(value, axis, [(i, (i + by) % size) for i in range(size)])  10.3 us
    unnamed x36, local copies, waits for them, and re-layouts  8.4 us
    all_to_all x1, starting transfers between devices, local(): a0 = lax.all_to_all(picked, 'pool', split_axis=0, concat_axis=0, tiled=True)  8.11 us
    ppermute x6, waiting for transfers between devices, shift(): lax.ppermute(value, axis, [(i, (i + by) % size) for i in range(size)])  5.33 us
  transfers between devices with their start and end apart: 12, of which 4 were waited for; matrix products, arithmetic and copies ran while one was open for 1% of the time, Pallas kernels for 12%

profile of v1, /device:TPU:64, one launch (start us, length us, event | category | flops | bytes accessed | tf_op | source)
XLA Modules:
  0.0 113.1 jit_solution(1313904349854631715)
XLA Ops:
  0.7 3.9 %pick_blocks.1 = (bf16[8,32,1152]{2,1,0:T(8,128)(2,1)}, bf16[160,768]{1,0:T(8,128)(2,1)}) custom-call(s32[3]{0:T(128)} %pad_add_fusion.ids, s32[2,8]{1,0:T(2,128)} %bitcast.7, bf16[16,73728]{1,0:T(8,128)(2,1)} %cache_ref.1, s32[8,64]{1,0:T(8,128)} %holder.3, s32[8,64]{1,0:T(8,128)} %block_ref.1, bf16[160,512]{1,0:T(8,128)(2,1)} %nope_ref.1, ...), custom_call_target="tpu_custom_call" | custom-call | tf_op jit(solution)/shard_map/pick_blocks/pallas_call | solution.py:472
  4.6 8.1 %all-to-all-start = ((bf16[8,32,1152]{2,1,0:T(8,128)(2,1)}), bf16[8,32,1152]{2,1,0:T(8,128)(2,1)}, u32[]{:S(2)}, u32[]{:S(2)}) async-start(bf16[8,32,1152]{2,1,0:T(8,128)(2,1)} %get-tuple-element.30), calls=%async_computation | async-start | bytes 1179648 | tf_op jit(solution)/shard_map/all_to_all | solution.py:499
  12.7 1.5 %collective-permute-start = (bf16[160,768]{1,0:T(8,128)(2,1)}, bf16[160,768]{1,0:T(8,128)(2,1)S(1)}, u32[]{:S(2)}, u32[]{:S(2)}) collective-permute-start(bf16[160,768]{1,0:T(8,128)(2,1)} %get-tuple-element.34.refs_0_), channel_id=1, source_target_pairs={{0,8},{8,16},{16,24},{24,0},{1,9},{9,17},{17,25},{25,1},{2,10},{10... | collective-permute-start | bytes 737288 | tf_op jit(solution)/shard_map/ppermute | solution.py:376
  14.2 1.7 %collective-permute-start.1 = (bf16[160,768]{1,0:T(8,128)(2,1)}, bf16[160,768]{1,0:T(8,128)(2,1)S(1)}, u32[]{:S(2)}, u32[]{:S(2)}) collective-permute-start(bf16[160,768]{1,0:T(8,128)(2,1)} %get-tuple-element.34.refs_0_), channel_id=1, source_target_pairs={{0,24},{8,0},{16,8},{24,16},{1,25},{9,1},{17,9},{25,17},{2,26},{10... | collective-permute-start | bytes 737288 | tf_op jit(solution)/shard_map/ppermute | solution.py:376
  16.0 5.3 %collective-permute-done.refs_0_ = bf16[160,768]{1,0:T(8,128)(2,1)S(1)} collective-permute-done((bf16[160,768]{1,0:T(8,128)(2,1)}, bf16[160,768]{1,0:T(8,128)(2,1)S(1)}, u32[]{:S(2)}, u32[]{:S(2)}) %collective-permute-start) | collective-permute-done | bytes 245792 | tf_op jit(solution)/shard_map/ppermute | solution.py:376
  21.3 1.6 %collective-permute-start.2 = (bf16[80,768]{1,0:T(8,128)(2,1)S(1)}, bf16[80,768]{1,0:T(8,128)(2,1)S(1)}, u32[]{:S(2)}, u32[]{:S(2)}) collective-permute-start(bf16[80,768]{1,0:T(8,128)(2,1)S(1)} %slice.12), channel_id=1, source_target_pairs={{0,8},{8,16},{16,24},{24,0},{1,9},{9,17},{17,25},{25,1},{2,10},{10... | collective-permute-start | bytes 368648 | tf_op jit(solution)/shard_map/ppermute | solution.py:376
  22.9 2.2 %collective-permute-start.3 = (bf16[80,768]{1,0:T(8,128)(2,1)S(1)}, bf16[80,768]{1,0:T(8,128)(2,1)S(1)}, u32[]{:S(2)}, u32[]{:S(2)}) collective-permute-start(bf16[80,768]{1,0:T(8,128)(2,1)S(1)} %slice.13), channel_id=1, source_target_pairs={{0,24},{8,0},{16,8},{24,16},{1,25},{9,1},{17,9},{25,17},{2,26},{10... | collective-permute-start | bytes 368648 | tf_op jit(solution)/shard_map/ppermute | solution.py:376
  25.1 0.9 copy-done.15
  26.0 5.7 %prepare_own.1 = (bf16[4,640,768]{2,1,0:T(8,128)(2,1)}, f32[4,640,512]{2,1,0:T(8,128)}, f32[4,640,128]{2,1,0:T(8,128)}, f32[4,640,128]{2,1,0:T(8,128)}, bf16[2048,128]{1,0:T(8,128)(2,1)}, /*index=5*/s32[32]{0:T(128)S(1)}) custom-call(s32[3]{0:T(128)S(1)} %copy-done.9, s32[8,64]{1,0:T(8,128)S(1)} %copy-done.8, s32[2,8]{1,0:T(2,128)S(1)} %bitcast.8, ...), custom_call_target="tpu_custom_call" | custom-call | flops 1000000000 | bytes 4000000 | tf_op jit(solution)/shard_map/prepare_own/pallas_call | solution.py:404
  32.4 1.1 fusion
  33.5 1.7 %collective-permute-start.4 = (bf16[4,32,1152]{2,1,0:T(8,128)(2,1)S(1)}, bf16[4,32,1152]{2,1,0:T(8,128)(2,1)}, u32[]{:S(2)}, u32[]{:S(2)}) collective-permute-start(bf16[4,32,1152]{2,1,0:T(8,128)(2,1)S(1)} %get-tuple-element.60), channel_id=1, source_target_pairs={{0,2},{1,3},{2,4},{3,5},{4,6},{5,7},{6,0},{7,1},{8,10},{9,11},{10,... | collective-permute-start | bytes 884744 | tf_op jit(solution)/shard_map/ppermute | solution.py:376
  35.1 1.7 %collective-permute-start.5 = (bf16[4,32,1152]{2,1,0:T(8,128)(2,1)S(1)}, bf16[4,32,1152]{2,1,0:T(8,128)(2,1)}, u32[]{:S(2)}, u32[]{:S(2)}) collective-permute-start(bf16[4,32,1152]{2,1,0:T(8,128)(2,1)S(1)} %get-tuple-element.59), channel_id=1, source_target_pairs={{0,6},{1,7},{2,0},{3,1},{4,2},{5,3},{6,4},{7,5},{8,14},{9,15},{10,... | collective-permute-start | bytes 884744 | tf_op jit(solution)/shard_map/ppermute | solution.py:376
  36.8 0.9 copy-done.1
  37.7 1.0 copy-done.3
  40.6 6.8 %prepare_others.1 = (bf16[4,640,768]{2,1,0:T(8,128)(2,1)}, f32[4,640,512]{2,1,0:T(8,128)}, f32[4,640,128]{2,1,0:T(8,128)}, f32[4,640,128]{2,1,0:T(8,128)}) custom-call(s32[3]{0:T(128)S(1)} %copy-done.9, s32[8,64]{1,0:T(8,128)S(1)} %copy-done.8, s32[2,8]{1,0:T(2,128)S(1)} %bitcast.9, ...), custom_call_target="tpu_custom_call", output_to_operand_aliasing={{0}: (10, {}), {1}: (11, {}), {2}: (12, {}), {3}: (13, {})} | custom-call | flops 3000000000 | bytes 12000000 | tf_op jit(solution)/shard_map/prepare_others/pallas_call | solution.py:404
  48.8 1.3 %collective-permute-done.7.bm = bf16[4,32,1152]{2,1,0:T(8,128)(2,1)S(1)} collective-permute-done((bf16[4,32,1152]{2,1,0:T(8,128)(2,1)}, bf16[4,32,1152]{2,1,0:T(8,128)(2,1)S(1)}, u32[]{:S(2)}, u32[]{:S(2)}) %collective-permute-start.7) | collective-permute-done | bytes 294944 | tf_op jit(solution)/shard_map/ppermute | solution.py:380
  50.6 1.1 copy-done.13
  51.7 1.0 copy-done.14
  52.8 19.6 %attend.1 = bf16[4,176,512]{2,1,0:T(8,128)(2,1)S(1)} custom-call(s32[3]{0:T(128)S(1)} %copy-done.9, s32[32]{0:T(128)S(1)} %get-tuple-element.36.table, bf16[4,640,768]{2,1,0:T(8,128)(2,1)} %get-tuple-element.45.q_ref, f32[4,640,512]{2,1,0:T(8,128)} %get-tuple-element.46.acc0, f32[4,640,128]{2,1,0:T(8,128)} %get-tuple-element.47.mx0, ...), custom_call_target="tpu_custom_call" | custom-call | flops 12000000000 | bytes 15000000 | tf_op jit(solution)/shard_map/attend/pallas_call | solution.py:433
  73.5 14.8 %all_to_all.15.got_ref = bf16[4,176,512]{2,1,0:T(8,128)(2,1)S(1)} all-to-all(bf16[4,176,512]{2,1,0:T(8,128)(2,1)S(1)} %attend.1), channel_id=1, replica_groups=mesh['pool'=8,'ctx'=4,'head'=8] {'ctx'}, dimensions={0} | all-to-all | bytes 1441792 | tf_op jit(solution)/shard_map/all_to_all | solution.py:521
  89.2 1.4 %collective-permute-done.9.other_ref = bf16[160,512]{1,0:T(8,128)(2,1)S(1)} collective-permute-done((bf16[160,512]{1,0:T(8,128)(2,1)S(1)}, bf16[160,512]{1,0:T(8,128)(2,1)S(1)}, u32[]{:S(2)}, u32[]{:S(2)}) %collective-permute-start.9) | collective-permute-done | bytes 163872 | tf_op jit(solution)/shard_map/ppermute | solution.py:380
  90.6 2.1 %project.1 = bf16[4,160,896]{2,1,0:T(8,128)(2,1)S(1)} custom-call(s32[3]{0:T(128)S(1)} %copy-done.9, bf16[160,512]{1,0:T(8,128)(2,1)S(1)} %merge.1.head_ref, bf16[160,512]{1,0:T(8,128)(2,1)S(1)} %collective-permute-done.9.other_ref, bf16[512,7168]{1,0:T(8,128)(2,1)S(1)} %bitcast.6, bf16[512,3584]{1,0:T(8,128)(2,1)S(1)} %collective-permute-done.10.x_ref), custom_call_target="tpu_custom_call" | custom-call | tf_op jit(solution)/shard_map/project/pallas_call | solution.py:536
  92.7 19.5 %all_to_all.16 = bf16[4,160,896]{2,1,0:T(8,128)(2,1)S(1)} all-to-all(bf16[4,160,896]{2,1,0:T(8,128)(2,1)S(1)} %project.1), channel_id=1, replica_groups={{0,2,4,6},{1,3,5,7},{8,10,12,14},{9,11,13,15},{16,18,20,22},{17,19,21,2..., dimensions={0} | all-to-all | bytes 2293760 | tf_op jit(solution)/shard_map/all_to_all | solution.py:547
  112.2 0.9 reduce_sum.12
  (52 shorter events, 7.2 us)
Async XLA Ops:
  0.0 25.1 %copy-start.10 = (s32[8,2]{0,1:T(2,128)S(1)}, s32[8,2]{0,1:T(2,128)}, u32[]{:S(2)}) copy-start(s32[8,2]{0,1:T(2,128)} %param.17) | copy-start | bytes 196
  0.0 25.1 %copy-start.8 = (s32[8,64]{1,0:T(8,128)S(1)}, s32[8,64]{1,0:T(8,128)}, u32[]{:S(2)}) copy-start(s32[8,64]{1,0:T(8,128)} %holder.3) | copy-start | bytes 6148
  0.0 25.1 %copy-start.11 = (s32[8,2]{0,1:T(2,128)S(1)}, s32[8,2]{0,1:T(2,128)}, u32[]{:S(2)}) copy-start(s32[8,2]{0,1:T(2,128)} %param.18) | copy-start | bytes 196
  0.0 25.1 %copy-start.4 = (bf16[80,1152]{1,0:T(8,128)(2,1)S(1)}, bf16[80,1152]{1,0:T(8,128)(2,1)}, u32[]{:S(2)}) copy-start(bf16[80,1152]{1,0:T(8,128)(2,1)} %refs_5_.1) | copy-start | bytes 552964
  0.0 25.0 %copy-start.2 = (bf16[4,128,512]{2,1,0:T(8,128)(2,1)S(1)}, bf16[4,128,512]{2,1,0:T(8,128)(2,1)}, u32[]{:S(2)}) copy-start(bf16[4,128,512]{2,1,0:T(8,128)(2,1)} %refs_4_.1) | copy-start | bytes 1572868
  0.7 24.4 %copy-start.9 = (s32[3]{0:T(128)S(1)}, s32[3]{0:T(128)}, u32[]{:S(2)}) copy-start(s32[3]{0:T(128)} %pad_add_fusion.ids) | copy-start | bytes 40
  4.6 27.7 %all-to-all-start = ((bf16[8,32,1152]{2,1,0:T(8,128)(2,1)}), bf16[8,32,1152]{2,1,0:T(8,128)(2,1)}, u32[]{:S(2)}, u32[]{:S(2)}) async-start(bf16[8,32,1152]{2,1,0:T(8,128)(2,1)} %get-tuple-element.30), calls=%async_computation | async-start | bytes 1179648 | tf_op jit(solution)/shard_map/all_to_all | solution.py:499
  12.7 8.6 %collective-permute-start = (bf16[160,768]{1,0:T(8,128)(2,1)}, bf16[160,768]{1,0:T(8,128)(2,1)S(1)}, u32[]{:S(2)}, u32[]{:S(2)}) collective-permute-start(bf16[160,768]{1,0:T(8,128)(2,1)} %get-tuple-element.34.refs_0_), channel_id=1, source_target_pairs={{0,8},{8,16},{16,24},{24,0},{1,9},{9,17},{17,25},{25,1},{2,10},{10... | collective-permute-start | bytes 737288 | tf_op jit(solution)/shard_map/ppermute | solution.py:376
  14.2 7.1 %collective-permute-start.1 = (bf16[160,768]{1,0:T(8,128)(2,1)}, bf16[160,768]{1,0:T(8,128)(2,1)S(1)}, u32[]{:S(2)}, u32[]{:S(2)}) collective-permute-start(bf16[160,768]{1,0:T(8,128)(2,1)} %get-tuple-element.34.refs_0_), channel_id=1, source_target_pairs={{0,24},{8,0},{16,8},{24,16},{1,25},{9,1},{17,9},{25,17},{2,26},{10... | collective-permute-start | bytes 737288 | tf_op jit(solution)/shard_map/ppermute | solution.py:376
  21.3 1.6 %copy-start = (bf16[160,768]{1,0:T(8,128)(2,1)}, bf16[160,768]{1,0:T(8,128)(2,1)S(1)}, u32[]{:S(2)}) copy-start(bf16[160,768]{1,0:T(8,128)(2,1)S(1)} %collective-permute-done.1.refs_1_) | copy-start | bytes 737284
  21.3 10.4 %collective-permute-start.2 = (bf16[80,768]{1,0:T(8,128)(2,1)S(1)}, bf16[80,768]{1,0:T(8,128)(2,1)S(1)}, u32[]{:S(2)}, u32[]{:S(2)}) collective-permute-start(bf16[80,768]{1,0:T(8,128)(2,1)S(1)} %slice.12), channel_id=1, source_target_pairs={{0,8},{8,16},{16,24},{24,0},{1,9},{9,17},{17,25},{25,1},{2,10},{10... | collective-permute-start | bytes 368648 | tf_op jit(solution)/shard_map/ppermute | solution.py:376
  22.9 8.8 %collective-permute-start.3 = (bf16[80,768]{1,0:T(8,128)(2,1)S(1)}, bf16[80,768]{1,0:T(8,128)(2,1)S(1)}, u32[]{:S(2)}, u32[]{:S(2)}) collective-permute-start(bf16[80,768]{1,0:T(8,128)(2,1)S(1)} %slice.13), channel_id=1, source_target_pairs={{0,24},{8,0},{16,8},{24,16},{1,25},{9,1},{17,9},{25,17},{2,26},{10... | collective-permute-start | bytes 368648 | tf_op jit(solution)/shard_map/ppermute | solution.py:376
  32.4 15.0 %collective-permute-start.6 = (bf16[8,32,1152]{2,1,0:T(8,128)(2,1)}, bf16[8,32,1152]{2,1,0:T(8,128)(2,1)S(1)}, u32[]{:S(2)}, u32[]{:S(2)}) collective-permute-start(bf16[8,32,1152]{2,1,0:T(8,128)(2,1)} %all-to-all-done.a0), channel_id=1, source_target_pairs={{0,1},{1,0},{2,3},{3,2},{4,5},{5,4},{6,7},{7,6},{8,9},{9,8},{10,11... | collective-permute-start | bytes 1769480 | tf_op jit(solution)/shard_map/ppermute | solution.py:380
  33.5 13.9 %collective-permute-start.4 = (bf16[4,32,1152]{2,1,0:T(8,128)(2,1)S(1)}, bf16[4,32,1152]{2,1,0:T(8,128)(2,1)}, u32[]{:S(2)}, u32[]{:S(2)}) collective-permute-start(bf16[4,32,1152]{2,1,0:T(8,128)(2,1)S(1)} %get-tuple-element.60), channel_id=1, source_target_pairs={{0,2},{1,3},{2,4},{3,5},{4,6},{5,7},{6,0},{7,1},{8,10},{9,11},{10,... | collective-permute-start | bytes 884744 | tf_op jit(solution)/shard_map/ppermute | solution.py:376
  35.1 12.3 %collective-permute-start.5 = (bf16[4,32,1152]{2,1,0:T(8,128)(2,1)S(1)}, bf16[4,32,1152]{2,1,0:T(8,128)(2,1)}, u32[]{:S(2)}, u32[]{:S(2)}) collective-permute-start(bf16[4,32,1152]{2,1,0:T(8,128)(2,1)S(1)} %get-tuple-element.59), channel_id=1, source_target_pairs={{0,6},{1,7},{2,0},{3,1},{4,2},{5,3},{6,4},{7,5},{8,14},{9,15},{10,... | collective-permute-start | bytes 884744 | tf_op jit(solution)/shard_map/ppermute | solution.py:376
  37.7 1.0 copy-start.3
  40.6 31.8 %slice-start = ((s8[7340032]{0:T(1024)(128)(4,1)}), s8[3145728]{0:T(1024)(128)(4,1)S(1)}, s32[]{:S(2)}) async-start(s8[7340032]{0:T(1024)(128)(4,1)} %bitcast.5), calls=%async_computation.3 | async-start | bytes 6291456
  48.3 1.8 %collective-permute-start.7 = (bf16[4,32,1152]{2,1,0:T(8,128)(2,1)}, bf16[4,32,1152]{2,1,0:T(8,128)(2,1)S(1)}, u32[]{:S(2)}, u32[]{:S(2)}) collective-permute-start(bf16[4,32,1152]{2,1,0:T(8,128)(2,1)} %collective-permute-done.4.am), channel_id=1, source_target_pairs={{0,1},{1,0},{2,3},{3,2},{4,5},{5,4},{6,7},{7,6},{8,9},{9,8},{10,11... | collective-permute-start | bytes 884744 | tf_op jit(solution)/shard_map/ppermute | solution.py:380
  48.4 2.3 %collective-permute-start.8 = (bf16[4,32,1152]{2,1,0:T(8,128)(2,1)}, bf16[4,32,1152]{2,1,0:T(8,128)(2,1)}, u32[]{:S(2)}, u32[]{:S(2)}) collective-permute-start(bf16[4,32,1152]{2,1,0:T(8,128)(2,1)} %collective-permute-done.5.ap), channel_id=1, source_target_pairs={{0,1},{1,0},{2,3},{3,2},{4,5},{5,4},{6,7},{7,6},{8,9},{9,8},{10,11... | collective-permute-start | bytes 884744 | tf_op jit(solution)/shard_map/ppermute | solution.py:380
  50.6 1.1 copy-start.13
  51.7 1.0 copy-start.14
  52.7 19.6 %slice-start.1 = ((s8[7340032]{0:T(1024)(128)(4,1)}), s8[4194304]{0:T(1024)(128)(4,1)S(1)}, s32[]{:S(2)}) async-start(s8[7340032]{0:T(1024)(128)(4,1)} %bitcast.5), calls=%async_computation.4 | async-start | bytes 8388608
  73.3 17.3 %collective-permute-start.10 = (bf16[512,3584]{1,0:T(8,128)(2,1)S(1)}, bf16[512,3584]{1,0:T(8,128)(2,1)S(1)}, u32[]{:S(2)}, u32[]{:S(2)}) collective-permute-start(bf16[512,3584]{1,0:T(8,128)(2,1)S(1)} %pad_maximum_fusion), channel_id=1, source_target_pairs={{0,1},{1,0},{2,3},{3,2},{4,5},{5,4},{6,7},{7,6},{8,9},{9,8},{10,11... | collective-permute-start | bytes 11010056 | tf_op jit(solution)/shard_map/ppermute | solution.py:380
  89.1 1.5 %collective-permute-start.9 = (bf16[160,512]{1,0:T(8,128)(2,1)S(1)}, bf16[160,512]{1,0:T(8,128)(2,1)S(1)}, u32[]{:S(2)}, u32[]{:S(2)}) collective-permute-start(bf16[160,512]{1,0:T(8,128)(2,1)S(1)} %merge.1.head_ref), channel_id=1, source_target_pairs={{0,1},{1,0},{2,3},{3,2},{4,5},{5,4},{6,7},{7,6},{8,9},{9,8},{10,11... | collective-permute-start | bytes 491528 | tf_op jit(solution)/shard_map/ppermute | solution.py:380
  (6 other events, 5.2 us)
